TPU v7x, 32 devices: a whole 2x2x4 slice. The times are simulated.
32 devices in a mesh: dp: 4 (over y, x), seq: 8 (over z, core).
Axes of the slice: x: 2, y: 2, z: 4, core: 2. Of those that a mesh axis runs over, the one named last changes fastest.
Arguments:
- char_ids: int32 [4, 4096], P('dp', 'seq'), may hold values from 0 to 255
- seg_starts: int32 [4, 8], P('dp', 'seq'), may hold values from 0 to 1, as said below
- char_table: bfloat16 [256, 1024], replicated, may hold values from -6 to 6
- norm_gain: float32 [1024], replicated, may hold values from 0.5 to 1.5
- qkv_weight: bfloat16 [1024, 3072], replicated, may hold values from -0.1875 to 0.1875
- distance_bias: float32 [256], replicated, may hold values from -3 to 3
- state_query: bfloat16 [512, 1024], replicated, may hold values from -9 to 9
- state_init: bfloat16 [512, 1024], replicated, may hold values from -6 to 6
- state_gain: float32 [1024], replicated, may hold values from 0.5 to 1.5
- state_kv_weight: bfloat16 [1024, 2048], replicated, may hold values from -0.1875 to 0.1875
- gate_logit: float32 [1024], replicated, may hold values from 0 to 6
- out_weight: bfloat16 [1024, 1024], replicated, may hold values from -1.5 to 1.5
- mlp_gain: float32 [1024], replicated, may hold values from 0.5 to 1.5
- up_weight: bfloat16 [1024, 4096], replicated, may hold values from -0.1875 to 0.1875
- down_weight: bfloat16 [4096, 1024], replicated, may hold values from -0.1875 to 0.1875
- cotangent: bfloat16 [4, 4096, 1024], P('dp', 'seq'), may hold values from -6 to 6
Outputs:
- layer_out: bfloat16 [4, 4096, 1024], P('dp', 'seq')
- grad_table: float32 [256, 1024], P('seq')
- grad_norm_gain: float32 [1024], P('seq')
- grad_qkv: float32 [1024, 3072], P('seq')
- grad_distance_bias: float32 [256], P('seq')
- grad_state_query: float32 [512, 1024], P('seq')
- grad_state_init: float32 [512, 1024], P('seq')
- grad_state_gain: float32 [1024], P('seq')
- grad_state_kv: float32 [1024, 2048], P('seq')
- grad_gate: float32 [1024], P('seq')
- grad_out: float32 [1024, 1024], P('seq')
- grad_mlp_gain: float32 [1024], P('seq')
- grad_up: float32 [1024, 4096], P('seq')
- grad_down: float32 [4096, 1024], P('seq')
Inputs may be any that keep to these rules, and one draw needn't show every extreme that they name: `seg_starts`: the first window of every row is marked; one of the 4 rows has no other mark.
All inputs are finite; a program needn't handle non-finite values.
Results may differ from a plain program's by a relative error of at most 0.034.
Values may be sent and summed in bfloat16 or wider, within the bound.
No kernel may reach another device: no remote copies, remote signals or barrier semaphores. Data moves between devices by JAX's collectives and lax.ppermute only.
A program may use at most 448 MiB of HBM per device.

v0:
```python
import functools
import math
import types

import jax
import jax.numpy as jnp
import numpy as np
from jax import lax
from jax.experimental import pallas as pl
from jax.experimental.pallas import tpu as pltpu
from jax.sharding import PartitionSpec as P

D = 1024
HEADS = 8
HEAD_DIM = 128
FF = 4096
VOCAB = 256
STATES = 512
WINDOW = 512
BUCKETS = 32
MAX_DISTANCE = 128
CONTEXT = 2 * WINDOW
TILE = 256
SPLITS = 2

epsilon = 1e-05
hidden = -1e30
log2e = math.log2(math.e)
score_scale = 1.0 / math.sqrt(HEAD_DIM)
f32 = jnp.float32
bf16 = jnp.bfloat16

NN = (((1,), (0,)), ((), ()))
NT = (((1,), (1,)), ((), ()))
TN = (((0,), (0,)), ((), ()))


def dot(a, b, dims=NN):
    return lax.dot_general(a, b, dims, preferred_element_type=f32)


def params(mib=26):
    return pltpu.CompilerParams(
        dimension_semantics=("arbitrary",), vmem_limit_bytes=mib * 1024 * 1024
    )


def cost(flops, moved, exps=0):
    return pl.CostEstimate(
        flops=int(flops), bytes_accessed=int(moved), transcendentals=int(exps)
    )


def norm_parts(value):
    centre = jnp.mean(value, axis=-1, keepdims=True)
    offset = value - centre
    spread = jnp.mean(offset * offset, axis=-1, keepdims=True)
    inv = lax.rsqrt(spread + epsilon)
    return offset * inv, inv


def norm_back(unit, inv, gain, upstream):
    scaled = upstream * gain
    a = jnp.mean(scaled, axis=-1, keepdims=True)
    b = jnp.mean(scaled * unit, axis=-1, keepdims=True)
    return (scaled - a - unit * b) * inv


def bucket_table():
    distance = np.arange(WINDOW)
    exact_count = BUCKETS // 2
    log_ratio = np.log(np.maximum(distance, 1) / exact_count) / math.log(
        MAX_DISTANCE / exact_count
    )
    far_bucket = exact_count + np.floor(log_ratio * (BUCKETS - exact_count)).astype(
        np.int64
    )
    return np.where(
        distance < exact_count, distance, np.minimum(far_bucket, BUCKETS - 1)
    )


def lane_pick():
    pick = np.zeros((BUCKETS, CONTEXT), np.float32)
    table = bucket_table()
    for m in range(1, WINDOW + 1):
        pick[table[WINDOW - m], m] = 1.0
    return pick


def lane_hidden():
    m = np.arange(CONTEXT)
    return np.where((m >= 1) & (m <= WINDOW), 0.0, hidden).astype(np.float32)[None]


smallest_sum = 2.0**-80


def shared_exp(lg, there):
    peak = jnp.max(jnp.where(there > 0, lg, hidden), axis=1, keepdims=True)
    return jnp.exp2(jnp.minimum(lg - peak, 0.0)).astype(bf16)


def window_sides(v, n):
    return jnp.concatenate([v.astype(f32) * n, n], axis=1).astype(bf16)


def own_weights(lg, n_row):
    x = lg + jnp.where(n_row > 0, jnp.log2(jnp.maximum(n_row, 1.0)), hidden)
    p = jnp.exp2(x - jnp.max(x, axis=1, keepdims=True))
    return p / jnp.sum(p, axis=1, keepdims=True)


def characters_there(span, rows):
    return lax.fori_loop(
        span[0], span[1], lambda w, t: t + rows[w], jnp.zeros((1, VOCAB), f32)
    )


TOGETHER = 4


def lanes_of(i):
    return slice(i * HEAD_DIM, (i + 1) * HEAD_DIM)


def summary_forward_kernel(
    span, sq, kt, vt, counts, rows, init, forget, state_out, y_out, low_out, a_s, y_s
):
    heads = range(TOGETHER)
    f = forget[...]
    v = [vt[:, lanes_of(i)] for i in heads]

    def scores(i):
        return dot(sq[:, lanes_of(i)], kt[:, lanes_of(i)], NT) * (score_scale * log2e)

    def begin():
        a_s[...] = init[...].astype(f32)
        y_s[...] = jnp.zeros_like(y_s)

    def move(i, u):
        at = lanes_of(i)
        a = a_s[:, at]
        y_s[:, at] = a - u + f[:, at] * y_s[:, at]
        a_s[:, at] = u + f[:, at] * (a - u)

    begin()
    there = characters_there(span, rows)
    e = [shared_exp(scores(i), there) for i in heads]

    def step(w, low):
        n = counts[w]
        for i in heads:
            both = dot(e[i], window_sides(v[i], n))
            z = both[:, HEAD_DIM:]
            move(i, both[:, :HEAD_DIM] / jnp.maximum(z, smallest_sum))
            low = jnp.minimum(low, jnp.min(z.reshape(STATES // 8, 8, 128), axis=0))
        return low

    low = lax.fori_loop(span[0], span[1], step, jnp.full((8, 128), 1.0, f32))
    low_out[0] = low

    @pl.when(jnp.min(low) < smallest_sum)
    def _():
        begin()
        for i in heads:
            lg = scores(i)

            def slow(w, _):
                move(i, dot(own_weights(lg, rows[w]).astype(bf16), v[i]))
                return 0

            lax.fori_loop(span[0], span[1], slow, 0)

    state_out[...] = a_s[...]
    y_out[...] = y_s[...]


def summary_specs(windows):
    wide = TOGETHER * HEAD_DIM
    head = lambda k: (lambda h, s: (0, k * HEADS // TOGETHER + h))
    return [
        pl.BlockSpec((STATES, wide), head(0)),
        pl.BlockSpec((VOCAB, wide), head(1)),
        pl.BlockSpec((VOCAB, wide), head(2)),
        pl.BlockSpec((windows, VOCAB, 128), lambda h, s: (0, 0, 0)),
        pl.BlockSpec((windows, 1, VOCAB), lambda h, s: (0, 0, 0)),
        pl.BlockSpec((STATES, wide), head(0)),
        pl.BlockSpec((1, wide), head(0)),
    ]


def summary_forward(span, state_query, qkv_table, counts, rows, state_init, forget):
    states = pl.BlockSpec((STATES, TOGETHER * HEAD_DIM), lambda h, s: (0, h))
    return pl.pallas_call(
        summary_forward_kernel,
        grid_spec=pltpu.PrefetchScalarGridSpec(
            num_scalar_prefetch=1,
            grid=(HEADS // TOGETHER,),
            in_specs=summary_specs(counts.shape[0]),
            out_specs=[states, states, pl.BlockSpec((1, 8, 128), lambda h, s: (h, 0, 0))],
            scratch_shapes=[pltpu.VMEM((STATES, TOGETHER * HEAD_DIM), f32)] * 2,
        ),
        out_shape=[
            jax.ShapeDtypeStruct((STATES, D), f32),
            pltpu.HBM((STATES, D), f32),
            jax.ShapeDtypeStruct((HEADS // TOGETHER, 8, 128), f32),
        ],
        compiler_params=params(),
        cost_estimate=cost(1e3, 1e3),
        name="summary_forward",
    )(span, state_query, qkv_table, qkv_table, counts, rows, *stays(state_init), forget)


def summary_backward_kernel(span, sq, kt, vt, counts, rows, local, forget, low, *rest):
    g_out, gsq_out, ginit_out, g_s, gs_s, gv_s, gs16, e_s, e_t = rest[-9:]
    heads = range(TOGETHER)
    f = forget[...]
    v = [vt[:, lanes_of(i)] for i in heads]
    g_s[...] = local[...]
    gs_s[...] = jnp.zeros_like(gs_s)
    gv_s[...] = jnp.zeros_like(gv_s)
    first, here = span[0], span[1]
    fast = jnp.min(low[0]) >= smallest_sum

    def scores(i):
        return dot(sq[:, lanes_of(i)], kt[:, lanes_of(i)], NT) * (score_scale * log2e)

    def carried(i):
        at = lanes_of(i)
        g = g_s[:, at]
        fg = f[:, at] * g
        g_s[:, at] = fg
        return g - fg

    @pl.when(fast)
    def _():
        there = characters_there(span, rows)
        for i in heads:
            e = shared_exp(scores(i), there)
            e_s[i] = e
            e_t[i] = e.astype(f32).T.astype(bf16)
        lane = lax.broadcasted_iota(jnp.int32, (STATES, HEAD_DIM), 1)

        def step(t, _):
            w = here - 1 - t
            n = counts[w]
            for i in heads:
                sides = window_sides(v[i], n)
                both = dot(e_s[i], sides)
                part = 1.0 / both[:, HEAD_DIM:]
                gu = (carried(i) * part).astype(bf16)
                inner = gu.astype(f32) * (both[:, :HEAD_DIM] * part)
                inner = inner + pltpu.roll(inner, HEAD_DIM // 2, 1)
                high = inner.astype(bf16)
                tail = jnp.where(
                    lane < HEAD_DIM // 2, high.astype(f32), inner - high.astype(f32)
                )
                gs_s[i] += dot(
                    jnp.concatenate([gu, (-tail).astype(bf16)], axis=1), sides, NT
                )
                gv_s[i] += n * dot(e_t[i], gu)
            return 0

        lax.fori_loop(0, here - first, step, 0)
        for i in heads:
            gs16[i] = (gs_s[i] * e_s[i].astype(f32) * score_scale).astype(bf16)

    @pl.when(jnp.logical_not(fast))
    def _():
        for i in heads:
            lg = scores(i)

            def slow(t, _):
                w = here - 1 - t
                p = own_weights(lg, rows[w])
                gu = carried(i).astype(bf16)
                pd = p * dot(gu, v[i], NT)
                gs_s[i] += pd - p * jnp.sum(pd, axis=1, keepdims=True)
                gv_s[i] += dot(p.astype(bf16), gu, TN)
                return 0

            lax.fori_loop(0, here - first, slow, 0)
            gs16[i] = (gs_s[i] * score_scale).astype(bf16)

    for i in heads:
        gs = gs16[i]
        at = lanes_of(i)
        g_out[i, :, :128] = jnp.zeros((VOCAB, 128), bf16)
        g_out[i, :, 128:256] = dot(gs, sq[:, at], TN).astype(bf16)
        g_out[i, :, 256:] = gv_s[i].astype(bf16)
        gsq_out[:, at] = dot(gs, kt[:, at]).astype(bf16)
    ginit_out[...] = g_s[...].astype(bf16)


def summary_backward(
    span, state_query, qkv_table, counts, rows, local, forget, low, deps=(), half=None, onto=()
):
    start, steps = (0, HEADS // TOGETHER) if half is None else (half, 1)
    deps = (*deps, *onto)
    wide = TOGETHER * HEAD_DIM
    windows = counts.shape[0]
    head = lambda k: (lambda h, s: (0, k * HEADS // TOGETHER + start + h))
    first = lambda h, s: (start + h, 0, 0)
    states = pl.BlockSpec((STATES, wide), head(0))
    return pl.pallas_call(
        summary_backward_kernel,
        grid_spec=pltpu.PrefetchScalarGridSpec(
            num_scalar_prefetch=1,
            grid=(steps,),
            in_specs=[
                states,
                pl.BlockSpec((VOCAB, wide), head(1)),
                pl.BlockSpec((VOCAB, wide), head(2)),
                pl.BlockSpec((windows, VOCAB, 128), lambda h, s: (0, 0, 0)),
                pl.BlockSpec((windows, 1, VOCAB), lambda h, s: (0, 0, 0)),
                states,
                pl.BlockSpec((1, wide), head(0)),
                pl.BlockSpec((1, 8, 128), first),
            ]
            + [pl.BlockSpec(memory_space=pl.ANY)] * len(deps),
            out_specs=[pl.BlockSpec((TOGETHER, VOCAB, 384), first), states, states],
            scratch_shapes=[
                pltpu.VMEM((STATES, wide), f32),
                pltpu.VMEM((TOGETHER, STATES, VOCAB), f32),
                pltpu.VMEM((TOGETHER, VOCAB, HEAD_DIM), f32),
                pltpu.VMEM((TOGETHER, STATES, VOCAB), bf16),
                pltpu.VMEM((TOGETHER, STATES, VOCAB), bf16),
                pltpu.VMEM((TOGETHER, VOCAB, STATES), bf16),
            ],
        ),
        out_shape=[
            jax.ShapeDtypeStruct((HEADS, VOCAB, 384), bf16),
            jax.ShapeDtypeStruct((STATES, D), bf16),
            jax.ShapeDtypeStruct((STATES, D), bf16),
        ],
        input_output_aliases={9 + len(deps) - 3 + i: i for i in range(len(onto))},
        compiler_params=params(),
        cost_estimate=cost(1e3, 1e3),
        name="summary_backward",
    )(span, state_query, qkv_table, qkv_table, counts, rows, local, forget, low, *deps)


def each_head(kernel, heads, kinds, *refs):
    kinds = "w" * (len(refs) - len(kinds)) + kinds
    for i in range(heads):
        views = {
            "l": lambda r, i=i: r.at[:, lanes_of(i)],
            "b": lambda r, i=i: r.at[i : i + 1],
            "s": lambda r, i=i: r.at[i],
            "w": lambda r: r,
        }
        kernel(*(views[kind](r) for kind, r in zip(kinds, refs)))


def bias_tile(row):
    spread = jnp.broadcast_to(row, (TILE, CONTEXT))
    shifted = pltpu.roll(spread, 0, 1, stride=1, stride_axis=0)
    return shifted[:, : 3 * TILE].T


def attention_forward_kernel(
    live, pick, pick_t, qt, kt, vt, sk, sv, bias_row, mixed_out, lse_out, bias
):
    bias[...] = bias_tile(bias_row[0])
    prev_add = jnp.where(live[0] > 0, 0.0, hidden).astype(f32)
    keys = dot(pick[...], kt[...]).astype(bf16)
    values_t = dot(vt[...], pick_t[...], TN).astype(bf16)
    query = dot(pick[WINDOW:, :], qt[...]).astype(bf16)
    state_values_t = sv[...].astype(f32).T.astype(bf16)
    for j in range(WINDOW // TILE):
        q = query[j * TILE : (j + 1) * TILE]
        scores = []
        for rel in range(3):
            kt_i = j + rel
            s = (
                dot(keys[kt_i * TILE : (kt_i + 1) * TILE], q, NT)
                * (score_scale * log2e)
                + bias[rel * TILE : (rel + 1) * TILE]
            )
            if kt_i * TILE < WINDOW:
                s = s + prev_add
            scores.append(s)
        for st in range(STATES // TILE):
            scores.append(
                dot(sk[st * TILE : (st + 1) * TILE, :], q, NT) * (score_scale * log2e)
            )
        peak = functools.reduce(
            jnp.maximum, [jnp.max(s, axis=0, keepdims=True) for s in scores]
        )
        total = jnp.zeros((1, TILE), f32)
        out = jnp.zeros((HEAD_DIM, TILE), f32)
        for i, s in enumerate(scores):
            p = jnp.exp2(s - peak)
            total = total + jnp.sum(p, axis=0, keepdims=True)
            if i < 3:
                v = values_t[:, (j + i) * TILE : (j + i + 1) * TILE]
            else:
                v = state_values_t[:, (i - 3) * TILE : (i - 2) * TILE]
            out = out + dot(v, p.astype(bf16))
        out = out * (1.0 / total)
        mixed_out[j * TILE : (j + 1) * TILE, :] = out.T.astype(bf16)
        lse_out[0, :, j * TILE : (j + 1) * TILE] = peak + jnp.log2(total)


def attention_forward(live, pick, pick_t, qkv_table, sk, sv, bias_rows):
    heads, wide = 4, 4 * HEAD_DIM
    head = lambda k: (lambda h, s: (0, k * HEADS // heads + h))
    whole = lambda *shape: pl.BlockSpec(shape, lambda h, s: (0,) * len(shape))
    return pl.pallas_call(
        functools.partial(each_head, attention_forward_kernel, heads, "wwwlllllblbs"),
        grid_spec=pltpu.PrefetchScalarGridSpec(
            num_scalar_prefetch=1,
            grid=(HEADS // heads,),
            in_specs=[
                whole(CONTEXT, VOCAB),
                whole(VOCAB, CONTEXT),
                pl.BlockSpec((VOCAB, wide), head(0)),
                pl.BlockSpec((VOCAB, wide), head(1)),
                pl.BlockSpec((VOCAB, wide), head(2)),
                pl.BlockSpec((STATES, wide), head(0)),
                pl.BlockSpec((STATES, wide), head(1)),
                pl.BlockSpec((heads, 1, CONTEXT), lambda h, s: (h, 0, 0)),
            ],
            out_specs=[
                pl.BlockSpec((WINDOW, wide), head(0)),
                pl.BlockSpec((heads, 1, WINDOW), lambda h, s: (h, 0, 0)),
            ],
            scratch_shapes=[pltpu.VMEM((heads, 3 * TILE, TILE), f32)],
        ),
        out_shape=[
            jax.ShapeDtypeStruct((WINDOW, D), bf16),
            jax.ShapeDtypeStruct((HEADS, 1, WINDOW), f32),
        ],
        compiler_params=params(),
        cost_estimate=cost(1e3, 1e3),
        name="attention_forward",
    )(live, pick, pick_t, qkv_table, qkv_table, qkv_table, sk, sv, bias_rows)


def back_tile(s, dp, shift, inner):
    p = jnp.exp2(s - shift)
    return p, p * (dp - inner)


def state_backward_kernel(pick, qt, sk, sv, lse, mixed, grad, *rest):
    gsk_out, gsv_out, gq_out, inner_out = rest[-4:]
    query = dot(pick[WINDOW:, :], qt[...]).astype(bf16)
    state_keys_t = sk[...].astype(f32).T.astype(bf16)
    inner_all = jnp.sum(
        (mixed[...].astype(f32) * grad[...].astype(f32)).T, axis=0, keepdims=True
    )
    inner_out[0] = inner_all
    blocks = WINDOW // TILE
    gq = [jnp.zeros((HEAD_DIM, TILE), f32) for _ in range(blocks)]
    for st in range(STATES // TILE):
        at = slice(st * TILE, (st + 1) * TILE)
        gk = jnp.zeros((TILE, HEAD_DIM), f32)
        gv = jnp.zeros((TILE, HEAD_DIM), f32)
        for j in range(blocks):
            rows = slice(j * TILE, (j + 1) * TILE)
            p, gs = back_tile(
                dot(sk[at, :], query[rows], NT) * (score_scale * log2e),
                dot(sv[at, :], grad[rows, :], NT),
                lse[0, :, rows],
                inner_all[:, rows],
            )
            gs16 = gs.astype(bf16)
            gq[j] = gq[j] + dot(state_keys_t[:, at], gs16)
            gk = gk + dot(gs16, query[rows])
            gv = gv + dot(p.astype(bf16), grad[rows, :])
        gsk_out[at, :] = (gk * score_scale).astype(bf16)
        gsv_out[at, :] = gv.astype(bf16)
    for j in range(blocks):
        gq_out[0, :, j * TILE : (j + 1) * TILE] = gq[j]


def state_backward(pick, qkv_table, state_kv, lse, mixed, grad, deps=()):
    heads, wide = 4, 4 * HEAD_DIM
    head = lambda k: (lambda h: (0, k * HEADS // heads + h))
    tokens = pl.BlockSpec((WINDOW, wide), head(0))
    states = pl.BlockSpec((STATES, wide), head(0))
    row = pl.BlockSpec((heads, 1, WINDOW), lambda h: (h, 0, 0))
    return pl.pallas_call(
        functools.partial(
            each_head, state_backward_kernel, heads, "wlllbll" + "w" * len(deps) + "llbb"
        ),
        grid=(HEADS // heads,),
        in_specs=[
            pl.BlockSpec((CONTEXT, VOCAB), lambda h: (0, 0)),
            pl.BlockSpec((VOCAB, wide), head(0)),
            pl.BlockSpec((STATES, wide), head(0)),
            pl.BlockSpec((STATES, wide), head(1)),
            row,
            tokens,
            tokens,
        ]
        + [pl.BlockSpec(memory_space=pl.ANY)] * len(deps),
        out_specs=[
            states,
            states,
            pl.BlockSpec((heads, HEAD_DIM, WINDOW), lambda h: (h, 0, 0)),
            row,
        ],
        out_shape=[
            pltpu.HBM((STATES, D), bf16),
            pltpu.HBM((STATES, D), bf16),
            jax.ShapeDtypeStruct((HEADS, HEAD_DIM, WINDOW), f32),
            jax.ShapeDtypeStruct((HEADS, 1, WINDOW), f32),
        ],
        compiler_params=params(),
        cost_estimate=cost(1e3, 1e3),
        name="state_backward",
    )(pick, qkv_table, state_kv, state_kv, lse, mixed, grad, *deps)


def token_backward_kernel(
    live, pick, pick_t, qt, kt, vt, bias_row, lse, inner, grad, gq_in, buckets, *rest
):
    g_out, fold_out, bias, bias_grad = rest[-4:]
    bias[...] = bias_tile(bias_row[0])
    bias_grad[...] = jnp.zeros_like(bias_grad)
    prev_add = jnp.where(live[0] > 0, 0.0, hidden).astype(f32)
    both = dot(pick[...], jnp.concatenate([kt[...], vt[...]], axis=1)).astype(bf16)
    keys = both[:, :HEAD_DIM]
    values = both[:, HEAD_DIM:]
    keys_t = dot(kt[...], pick_t[...], TN).astype(bf16)
    query = dot(pick[WINDOW:, :], qt[...]).astype(bf16)
    blocks = WINDOW // TILE
    gq = [gq_in[0, :, j * TILE : (j + 1) * TILE] for j in range(blocks)]
    sums = jnp.zeros((VOCAB, 2 * HEAD_DIM), f32)
    for tile in range(CONTEXT // TILE):
        at = slice(tile * TILE, (tile + 1) * TILE)
        gk = jnp.zeros((TILE, HEAD_DIM), f32)
        gv = jnp.zeros((TILE, HEAD_DIM), f32)
        for j in range(blocks):
            rel = tile - j
            if not 0 <= rel < 3:
                continue
            rows = slice(j * TILE, (j + 1) * TILE)
            rels = slice(rel * TILE, (rel + 1) * TILE)
            shift = lse[0, :, rows]
            if tile * TILE < WINDOW:
                shift = shift - prev_add
            p, gs = back_tile(
                dot(keys[at], query[rows], NT) * (score_scale * log2e) + bias[rels],
                dot(values[at], grad[rows, :], NT),
                shift,
                inner[0, :, rows],
            )
            gs16 = gs.astype(bf16)
            gq[j] = gq[j] + dot(keys_t[:, at], gs16)
            bias_grad[rels] += gs
            gk = gk + dot(gs16, query[rows])
            gv = gv + dot(p.astype(bf16), grad[rows, :])
        pair = jnp.concatenate([gk * score_scale, gv], axis=1).astype(bf16)
        sums = sums + dot(pick_t[:, at], pair)
    g_out[0, :, HEAD_DIM:] = sums
    total = jnp.zeros((HEAD_DIM, VOCAB), f32)
    for j in range(blocks):
        rows = slice(WINDOW + j * TILE, WINDOW + (j + 1) * TILE)
        total = total + dot((gq[j] * score_scale).astype(bf16), pick[rows, :])
    g_out[0, :, :HEAD_DIM] = total.T
    rows = jnp.concatenate(
        [bias_grad[...].T, jnp.zeros((TILE, CONTEXT - 3 * TILE), f32)], axis=1
    )
    count = TILE
    while count > 8:
        count //= 2
        rows = rows[:count] + pltpu.roll(rows[count:], CONTEXT - count, 1)
    folded = rows[0:1]
    for r in range(1, 8):
        folded = folded + pltpu.roll(rows, CONTEXT - r, 1)[r : r + 1]
    pieces = []
    left = folded
    for _ in range(3):
        piece = left.astype(bf16)
        pieces.append(piece)
        left = left - piece.astype(f32)
    pieces = jnp.concatenate(pieces + [jnp.zeros((5, CONTEXT), bf16)], axis=0)
    fold_out[0] = jnp.sum(dot(pieces, buckets[...]), axis=0, keepdims=True)


def token_backward(
    live, pick, pick_t, qkv_table, bias_rows, lse, inner, grad, gq, deps=(), half=None, onto=()
):
    heads, wide = 4, 4 * HEAD_DIM
    count = HEADS // heads if half is None else HEADS // heads // 2
    low = 0 if half is None else half * count
    deps = (*deps, *onto)
    head = lambda k: (lambda h, s: (0, k * HEADS // heads + low + h))
    by_head = lambda *shape: pl.BlockSpec((heads,) + shape, lambda h, s: (low + h, 0, 0))
    flat = lambda *shape: pl.BlockSpec(shape, lambda h, s: (0,) * len(shape))
    return pl.pallas_call(
        functools.partial(
            each_head, token_backward_kernel, heads, "wwwlllbbblbw" + "w" * len(deps) + "bbss"
        ),
        grid_spec=pltpu.PrefetchScalarGridSpec(
            num_scalar_prefetch=1,
            grid=(count,),
            in_specs=[
                flat(CONTEXT, VOCAB),
                flat(VOCAB, CONTEXT),
                pl.BlockSpec((VOCAB, wide), head(0)),
                pl.BlockSpec((VOCAB, wide), head(1)),
                pl.BlockSpec((VOCAB, wide), head(2)),
                by_head(1, CONTEXT),
                by_head(1, WINDOW),
                by_head(1, WINDOW),
                pl.BlockSpec((WINDOW, wide), head(0)),
                by_head(HEAD_DIM, WINDOW),
                flat(CONTEXT, 128),
            ]
            + [pl.BlockSpec(memory_space=pl.ANY)] * len(deps),
            out_specs=[by_head(VOCAB, 384), by_head(1, 128)],
            scratch_shapes=[
                pltpu.VMEM((heads, 3 * TILE, TILE), f32),
                pltpu.VMEM((heads, 3 * TILE, TILE), f32),
            ],
        ),
        out_shape=[
            jax.ShapeDtypeStruct((HEADS, VOCAB, 384), f32),
            jax.ShapeDtypeStruct((HEADS, 1, 128), f32),
        ],
        input_output_aliases={12 + len(deps) - 2 + i: i for i in range(len(onto))},
        compiler_params=params(),
        cost_estimate=cost(1e3, 1e3),
        name="token_backward",
    )(
        live,
        pick,
        pick_t,
        qkv_table,
        qkv_table,
        qkv_table,
        bias_rows,
        lse,
        inner,
        grad,
        gq,
        jnp.asarray(np.pad(lane_pick().T, ((0, 0), (0, 96))), bf16),
        *deps,
    )


def mlp_kernel(x, cot, up, down, out_in, gx_in, gd_out, gu_out, out, gx, xt):
    @pl.when(pl.program_id(0) == 0)
    def _():
        out[...] = out_in[...]
        gx[...] = gx_in[...]
        xt[...] = x[...].astype(f32).T.astype(bf16)

    up_b = up[...]
    down_b = down[...]
    pre = dot(x[...], up_b)
    root = math.sqrt(2.0 / math.pi)
    square = pre * pre
    t = jnp.tanh(root * pre * (1.0 + 0.044715 * square))
    half = 0.5 * (1.0 + t)
    act = (pre * half).astype(bf16)
    slope = half + (0.5 * root) * pre * (1.0 - t * t) * (1.0 + (3 * 0.044715) * square)
    grad_pre = (dot(cot[...], down_b, NT) * slope).astype(bf16)
    out[...] += dot(act, down_b)
    gx[...] += dot(grad_pre, up_b, NT)
    gd_out[...] = dot(act, cot[...], TN).astype(bf16)
    gu_out[...] = dot(xt[...], grad_pre).astype(bf16)


def mlp_part(part, x, cot, up, down, out, gx):
    count = FF // SPLITS // TILE
    whole = pl.BlockSpec((WINDOW, D), lambda s: (0, 0))
    return pl.pallas_call(
        mlp_kernel,
        grid=(count,),
        in_specs=[
            whole,
            whole,
            pl.BlockSpec((D, TILE), lambda s: (0, SPLITS * s + part)),
            pl.BlockSpec((TILE, D), lambda s: (SPLITS * s + part, 0)),
            whole,
            whole,
        ],
        out_specs=[
            pl.BlockSpec((TILE, D), lambda s: (s, 0)),
            pl.BlockSpec((D, TILE), lambda s: (0, s)),
            whole,
            whole,
        ],
        out_shape=[
            jax.ShapeDtypeStruct((count * TILE, D), bf16),
            jax.ShapeDtypeStruct((D, count * TILE), bf16),
            jax.ShapeDtypeStruct((WINDOW, D), f32),
            jax.ShapeDtypeStruct((WINDOW, D), f32),
        ],
        scratch_shapes=[pltpu.VMEM((D, WINDOW), bf16)],
        compiler_params=params(),
        cost_estimate=cost(1e3, 1e3),
        name="feed_forward",
    )(x, cot, up, down, out, gx)


def mlp_packed_kernel(
    places, x, xs, cot, up_a, up_b, up_c, up_d, down_a, down_b, down_c, down_d, out_in, gx_in,
    *rest,
):
    send, keep, out, gx, gd_s = rest[-5:]
    core = places[CORE]
    step = pl.program_id(0)

    @pl.when(step == 0)
    def _():
        out[...] = out_in[...]
        gx[...] = gx_in[...]

    up = jnp.concatenate([up_a[...], up_b[...], up_c[...], up_d[...]], axis=1)
    down = jnp.concatenate([down_a[...], down_b[...], down_c[...], down_d[...]], axis=0)
    pre = dot(x[...], up)
    root = math.sqrt(2.0 / math.pi)
    square = pre * pre
    t = jnp.tanh(root * pre * (1.0 + 0.044715 * square))
    half = 0.5 * (1.0 + t)
    act = (pre * half).astype(bf16)
    slope = half + (0.5 * root) * pre * (1.0 - t * t) * (1.0 + (3 * 0.044715) * square)
    grad_pre = (dot(cot[...], down, NT) * slope).astype(bf16)
    out[...] += dot(act, down)
    gx[...] += dot(grad_pre, up, NT)
    gd = dot(act, cot[...], TN).astype(bf16)
    for i in range(2):
        for q in range(2):
            at = (2 * i + q) * 128
            gd_s[q, i] = gd[at : at + 128]
    lanes = pl.ds(pl.multiple_of(step * 512, 512), 512)
    for i in range(2):
        z = 2 * step + i
        send[pl.ds(z, 1), :128, :] = gd_s[pl.ds(1 - core, 1), i]
        keep[pl.ds(z, 1), :128, :] = gd_s[pl.ds(core, 1), i]
    for slot, ref in ((0, send), (1, keep)):
        gu = dot(xs[slot], grad_pre).astype(bf16)
        ref[:, 128:, lanes] = gu.reshape(4, 128, 512)


def mlp_packed(part, places, x, split, cot, up, down, out, gx, deps=()):
    block = pl.BlockSpec((WINDOW, D), lambda g, s: (0, 0))
    packed = pl.BlockSpec((4, 256, D), lambda g, s: (0, 0, 0))
    at = lambda k: (lambda g: (4 * g + k) * 4 + part)
    return pl.pallas_call(
        mlp_packed_kernel,
        grid_spec=pltpu.PrefetchScalarGridSpec(
            num_scalar_prefetch=1,
            grid=(2,),
            in_specs=[block, pl.BlockSpec((2, WINDOW, WINDOW), lambda g, s: (0, 0, 0)), block]
            + [
                pl.BlockSpec((D, 128), lambda g, s, k=k: (0, at(k)(g)))
                for k in range(4)
            ]
            + [
                pl.BlockSpec((128, D), lambda g, s, k=k: (at(k)(g), 0))
                for k in range(4)
            ]
            + [block, block]
            + [pl.BlockSpec(memory_space=pl.ANY)] * len(deps),
            out_specs=[packed, packed, block, block],
            scratch_shapes=[pltpu.VMEM((2, 2, 128, D), bf16)],
        ),
        out_shape=[
            jax.ShapeDtypeStruct((4, 256, D), bf16),
            jax.ShapeDtypeStruct((4, 256, D), bf16),
            jax.ShapeDtypeStruct((WINDOW, D), f32),
            jax.ShapeDtypeStruct((WINDOW, D), f32),
        ],
        compiler_params=params(32),
        cost_estimate=cost(1e3, 1e3),
        name="feed_forward",
    )(places, x, split, cot, up, up, up, up, down, down, down, down, out, gx, *deps)


def one_block(array):
    return pl.BlockSpec(array.shape, lambda g: (0,) * len(array.shape))


def single(kernel, name, ins, outs, scratch=(), deps=()):
    return pl.pallas_call(
        kernel,
        grid=(1,),
        in_specs=[one_block(a) for a in ins]
        + [pl.BlockSpec(memory_space=pl.ANY)] * len(deps),
        out_specs=[one_block(o) for o in outs],
        out_shape=list(outs),
        scratch_shapes=list(scratch),
        compiler_params=params(),
        cost_estimate=cost(1e3, 1e3),
        name=name,
    )(*ins, *deps)


def like(kind, *shape):
    return jax.ShapeDtypeStruct(shape, kind)


def kept(kind, *shape):
    return pltpu.HBM(shape, kind)


def stays(*arrays):
    return tuple(pltpu.with_memory_space_constraint(a, pltpu.HBM) for a in arrays)


def unit_of(value):
    unit, inv = norm_parts(value)
    return unit, jnp.broadcast_to(inv, (value.shape[0], 128))


def table_kernel(table, gain, weight, unit_out, inv_out, normed_out, qkv_out):
    step = pl.program_id(0)

    @pl.when(step == 0)
    def _():
        unit, inv = unit_of(table[...].astype(f32))
        unit_out[...] = unit
        inv_out[...] = inv
        normed_out[...] = (unit * gain[...]).astype(bf16)

    qkv_out[...] = dot(normed_out[...], weight[...]).astype(bf16)


def table_forward(table, gain, weight):
    flat = lambda *shape: pl.BlockSpec(shape, lambda g: (0, 0))
    return pl.pallas_call(
        table_kernel,
        grid=(6,),
        in_specs=[
            flat(VOCAB, D),
            flat(1, D),
            pl.BlockSpec((D, D // 2), lambda g: (0, g)),
        ],
        out_specs=[
            flat(VOCAB, D),
            flat(VOCAB, 128),
            flat(VOCAB, D),
            pl.BlockSpec((VOCAB, D // 2), lambda g: (0, g)),
        ],
        out_shape=[
            kept(f32, VOCAB, D),
            kept(f32, VOCAB, 128),
            kept(bf16, VOCAB, D),
            like(bf16, VOCAB, 3 * D),
        ],
        compiler_params=params(),
        cost_estimate=cost(1e3, 1e3),
        name="table_forward",
    )(*stays(table), gain, *stays(weight))


def states_forward_kernel(states, gain, weight, unit_out, inv_out, normed_out, kv_out):
    step = pl.program_id(0)

    @pl.when(step == 0)
    def _():
        unit, inv = unit_of(states[...])
        unit_out[...] = unit
        inv_out[...] = inv
        normed_out[...] = (unit * gain[...]).astype(bf16)

    kv_out[...] = dot(normed_out[...], weight[...]).astype(bf16)


def states_forward(states, gain, weight):
    flat = lambda *shape: pl.BlockSpec(shape, lambda g: (0, 0))
    return pl.pallas_call(
        states_forward_kernel,
        grid=(4,),
        in_specs=[
            flat(STATES, D),
            flat(1, D),
            pl.BlockSpec((D, D // 2), lambda g: (0, g)),
        ],
        out_specs=[
            flat(STATES, D),
            flat(STATES, 128),
            flat(STATES, D),
            pl.BlockSpec((STATES, D // 2), lambda g: (0, g)),
        ],
        out_shape=[
            kept(f32, STATES, D),
            kept(f32, STATES, 128),
            kept(bf16, STATES, D),
            like(bf16, STATES, 2 * D),
        ],
        compiler_params=params(),
        cost_estimate=cost(1e3, 1e3),
        name="states_forward",
    )(states, gain, weight)


def residual_kernel(
    places, mixed, out_weight, pick, table, gain, res_out, unit_out, inv_out, in_out, split_out, xt
):
    res = dot(pick[WINDOW:, :], table[...]) + dot(mixed[...], out_weight[...])
    res_out[...] = res
    unit, inv = unit_of(res)
    unit_out[...] = unit
    inv_out[...] = inv
    x = unit * gain[...]
    in_out[...] = x.astype(bf16)
    xt[...] = x.T.astype(bf16)
    core = places[CORE]
    for z in range(4):
        for slot, parity in ((0, 1 - core), (1, core)):
            at = pl.multiple_of((2 * z + parity) * 128, 128)
            split_out[slot, z * 128 : (z + 1) * 128, :] = xt[pl.ds(at, 128), :]


def residual_forward(places, *ins):
    outs = (
        like(f32, WINDOW, D),
        kept(f32, WINDOW, D),
        kept(f32, WINDOW, 128),
        like(bf16, WINDOW, D),
        like(bf16, 2, WINDOW, WINDOW),
    )
    return pl.pallas_call(
        residual_kernel,
        grid_spec=pltpu.PrefetchScalarGridSpec(
            num_scalar_prefetch=1,
            grid=(1,),
            in_specs=[whole(a) for a in ins],
            out_specs=[whole(o) for o in outs],
            scratch_shapes=[pltpu.VMEM((D, WINDOW), bf16)],
        ),
        out_shape=list(outs),
        compiler_params=params(),
        cost_estimate=cost(1e3, 1e3),
        name="residual_forward",
    )(places, *ins)


def feed_back_kernel(
    gx, unit, inv, gain, upstream, mixed, out_weight, pick, *rest
):
    gain_out, out_out, mixed_out, rows_out = rest[-4:]
    g = gx[...]
    u = unit[...]
    gain_out[...] = jnp.sum(g * u, axis=0, keepdims=True)
    back = norm_back(u, inv[:, :1], gain[...], g)
    grad = (upstream[...].astype(f32) + back).astype(bf16)
    mixed_out[...] = dot(grad, out_weight[...], NT).astype(bf16)
    out_out[...] = dot(mixed[...], grad, TN).astype(bf16)
    rows_out[...] = dot(pick[WINDOW:, :], grad, TN).astype(bf16)


def feed_back(v, gx, deps=()):
    return single(
        feed_back_kernel,
        "feed_back",
        (
            gx,
            v.mlp_unit,
            v.mlp_inv,
            v.mlp_gain,
            v.upstream,
            v.mixed,
            v.out_weight,
            v.pick,
        ),
        (like(f32, 1, D), like(bf16, D, D), like(bf16, WINDOW, D), like(bf16, VOCAB, D)),
        deps=deps,
    )


def states_back_kernel(
    gsk, gsv, weight, normed, unit, inv, gain, slope, forget, *rest
):
    k_out, v_out, gain_out, local_out, gate_out = rest[-5:]
    upstream = dot(gsk[...], weight[:, :D], NT) + dot(gsv[...], weight[:, D:], NT)
    u = unit[...]
    gain_out[...] = jnp.sum(upstream * u, axis=0, keepdims=True)
    local = norm_back(u, inv[:, :1], gain[...], upstream)
    local_out[...] = local
    f = forget[...]
    gate_out[...] = jnp.sum(local * slope[...], axis=0, keepdims=True) * f * (1.0 - f)
    k_out[...] = dot(normed[...], gsk[...], TN).astype(bf16)
    v_out[...] = dot(normed[...], gsv[...], TN).astype(bf16)


def states_back(v, gsk, gsv, deps=()):
    return single(
        states_back_kernel,
        "states_back",
        (
            *stays(gsk, gsv, v.state_kv_weight, v.state_normed, v.state_unit, v.state_inv),
            v.state_gain,
            *stays(v.forget_slope),
            v.forget,
        ),
        (
            like(bf16, D, D),
            like(bf16, D, D),
            like(f32, 1, D),
            like(f32, STATES, D),
            like(f32, 1, D),
        ),
        deps=deps,
    )


XI, YI, ZI, CORE, DPI, SEQI = range(6)


def permute(value, axis, to):
    size = lax.axis_size(axis)
    return lax.ppermute(value, axis, [(i, to(i)) for i in range(size)])


def swap_core(value):
    return permute(value, "seq", lambda i: i ^ 1)


def swap_dp(value, step):
    return permute(value, "dp", lambda i: i ^ step)


def ahead(value, step):
    return permute(value, "seq", lambda i: (i + 2 * step) % 8)


def fitted():
    return lax.axis_size("seq") == 8 and lax.axis_size("dp") == 4


def whole(array):
    return pl.BlockSpec(array.shape, lambda g, s: (0,) * len(array.shape))


def blend(name, places, outs, deps=(), through=()):
    arrays, in_specs, plan, out_specs = [], [], [], []
    for shape, rows, blocks, segments in outs:
        every = 4 // blocks
        rows_of = []
        for sources in segments:
            names = []
            for array, block_rows, place in sources:
                names.append(len(arrays))
                arrays.append(array)
                in_specs.append(
                    pl.BlockSpec(
                        (1, block_rows, array.shape[2]),
                        lambda g, s, place=place, every=every: (*place(g // every, s), 0),
                    )
                )
            rows_of.append((sources[0][1], names))
        plan.append((every, rows_of))
        out_specs.append(
            pl.BlockSpec((1, rows, shape[2]), lambda g, s, every=every: (g // every, 0, 0))
        )
    count = len(arrays)

    def kernel(s, *refs):
        step = pl.program_id(0)
        out_refs = refs[count + len(deps) + len(through) :]

        def fill(out_ref, rows_of):
            at = 0
            for rows, names in rows_of:
                total = refs[names[0]][0].astype(f32)
                for i in names[1:]:
                    total = total + refs[i][0].astype(f32)
                out_ref[0, at : at + rows, :] = total.astype(out_ref.dtype)
                at += rows

        for out_ref, (every, rows_of) in zip(out_refs, plan):
            if every == 1:
                fill(out_ref, rows_of)
            else:
                pl.when(step % every == 0)(functools.partial(fill, out_ref, rows_of))

    return pl.pallas_call(
        kernel,
        grid_spec=pltpu.PrefetchScalarGridSpec(
            num_scalar_prefetch=1,
            grid=(4,),
            in_specs=in_specs
            + [pl.BlockSpec(memory_space=pl.ANY)] * (len(deps) + len(through)),
            out_specs=out_specs + [pl.BlockSpec(memory_space=pl.ANY)] * len(through),
        ),
        out_shape=[jax.ShapeDtypeStruct(shape, bf16) for shape, _, _, _ in outs]
        + [jax.ShapeDtypeStruct(t.shape, t.dtype) for t in through],
        input_output_aliases={
            1 + count + len(deps) + i: len(outs) + i for i in range(len(through))
        },
        compiler_params=params(),
        cost_estimate=cost(1e3, 1e3),
        name=name,
    )(places, *arrays, *deps, *through)


class Wing:
    def __init__(self, lead, kept, came, base, rows):
        self.lead, self.trail = lead, 1 - lead
        self.kept, self.came, self.base = kept, came, base
        self.half, self.quarter = rows // 2, rows // 4
        self.columns = kept.shape[2]
        self.got = []

    def first(self):
        at = self.base // self.half
        other = lambda g, s: (g, at + 1 - s[self.lead])
        return self.half, [(self.kept, self.half, other), (self.came, self.half, other)]

    def second(self):
        q = self.quarter
        at = self.base // q
        array, start = self.got[0]
        start = start // q
        deep = lambda g, s: (g, at + 2 * s[self.lead] + 1 - s[self.trail])
        flat = lambda g, s: (g, start + 1 - s[self.trail])
        return q, [(self.kept, q, deep), (self.came, q, deep), (array, q, flat)]

    def quarters(self, level):
        q = self.quarter
        at = self.base // q
        (one, start_one), (two, start_two) = self.got
        start_one, start_two = start_one // q, start_two // q
        deep = lambda g, s: (level(g, s), at + 2 * s[self.lead] + s[self.trail])
        flat = lambda g, s: (level(g, s), start_one + s[self.trail])
        last = lambda g, s: (level(g, s), start_two)
        return [(self.kept, q, deep), (self.came, q, deep), (one, q, flat), (two, q, last)]


def wings(kept, came):
    half = kept.shape[1] // 2
    return [Wing(XI, kept, came, 0, half), Wing(YI, kept, came, half, half)]


class Column:
    def __init__(self, parts):
        self.parts = parts
        self.rows = sum(w.quarter for w in parts)
        self.columns = parts[0].columns

    def near(self):
        outs = []
        for own in (False, True):
            level = (
                (lambda g, s: 2 * g + s[ZI] % 2)
                if own
                else (lambda g, s: 2 * g + 1 - s[ZI] % 2)
            )
            segments = [w.quarters(level) for w in self.parts]
            outs.append(((2, self.rows, self.columns), self.rows, 2, segments))
        return outs

    def rest(self, pick, extra=()):
        sources = [
            (array, self.rows, lambda g, s: (pick(s), 0))
            for array in (self.kept, self.from_near)
        ] + [(array, self.rows, lambda g, s: (0, 0)) for array in extra]
        return [((1, self.rows, self.columns), self.rows, 1, [sources])]

    def far(self):
        return self.rest(lambda s: 1 - s[ZI] // 2)

    def close(self):
        return self.rest(lambda s: s[ZI] // 2, [self.from_far])


class Traffic:
    def __init__(self, places):
        self.places = places
        self.pending = []

    def swap(self, send):
        came = swap_core(send)
        self.pending.append(came)
        return came

    def boundary(self, after, first=(), second=(), near=(), far=(), close=(), swap=(), join=()):
        outs, sent = [], []
        for axis in (XI, YI):
            groups = {}
            for w in first:
                if w.lead == axis:
                    groups.setdefault(w.columns, []).append((w, w.first()))
            for w in second:
                if w.trail == axis:
                    groups.setdefault(w.columns, []).append((w, w.second()))
            for columns, moves in groups.items():
                moves.sort(key=lambda m: -m[1][0])
                rows = sum(m[1][0] for m in moves)
                outs.append(
                    ((4, rows, columns), rows, 4, [m[1][1] for m in moves])
                )
                sent.append((axis, moves))
        for columns, step in ((near, Column.near), (far, Column.far), (close, Column.close)):
            for c in columns:
                outs += step(c)
        if join:
            segments = [c.close()[0][3][0] for c in join]
            total = sum(c.rows for c in join)
            outs.append(((1, total, join[0].columns), total, 1, segments))
        results = blend("boundary", self.places, outs, (*after, *self.pending), swap)
        self.pending = []
        mark = results[0]
        results = list(results)
        for axis, moves in sent:
            came = swap_dp(results.pop(0), 1 << axis)
            self.pending.append(came)
            at = 0
            for w, (rows, _) in moves:
                assert at % w.quarter == 0
                w.got.append((came, at))
                at += rows
        for c in near:
            c.from_near = permute(results.pop(0), "seq", lambda i: i ^ 2)
            c.kept = results.pop(0)
            self.pending.append(c.from_near)
        for c in far:
            c.from_far = permute(results.pop(0), "seq", lambda i: i ^ 4)
            self.pending.append(c.from_far)
        for c in close:
            c.own = results.pop(0)
        if join:
            self.joined = results.pop(0)
        self.swapped = [self.swap(send) for send in results]
        return mark

    def spread(self, own, lead=1):
        beside = swap_dp(own, lead)
        other = swap_dp(own, 3 - lead)
        rows = [own, beside, other, swap_dp(beside, 3 - lead)]
        self.pending += rows[1:]
        return rows if lead == 1 else [own, other, beside, rows[3]]


def packed_pair(name, places, pieces, deps=()):
    rows = sum(p.shape[1] for p in pieces)
    columns = pieces[0].shape[2]
    outs = []
    for keep in (False, True):
        place = (
            (lambda g, s: (2 * g + s[CORE], 0))
            if keep
            else (lambda g, s: (2 * g + 1 - s[CORE], 0))
        )
        outs.append(
            ((4, rows, columns), rows, 4, [[(p, p.shape[1], place)] for p in pieces])
        )
    return blend(name, places, outs, deps)


def pack_rows(places, mark, g_tokens, g, rows_sum, *vectors):
    count = 3 + len(vectors)

    def kernel(s, *refs):
        for out_ref, (a, b, r, *rows) in zip(
            refs[2 * count + 1 :], (refs[:count], refs[count : 2 * count])
        ):
            out_ref[0, :VOCAB, :] = (a[0] + b[0].astype(f32)).astype(bf16)
            out_ref[0, VOCAB:, :128] = r[:128, :]
            out_ref[0, VOCAB:, 128:256] = r[128:, :]
            place = lax.broadcasted_iota(jnp.int32, (128, 128), 0)
            small = jnp.zeros((128, 128), f32)
            for i, row in enumerate(rows):
                value = row[...] if len(row.shape) == 2 else row[0]
                small = jnp.where(place == i, value, small)
            out_ref[0, VOCAB:, 256:] = small.astype(bf16)

    specs, arrays = [], []
    for keep in (False, True):
        at = (
            (lambda i, s: 2 * i + s[CORE]) if keep else (lambda i, s: 2 * i + 1 - s[CORE])
        )
        for array in (g_tokens, g, rows_sum, *vectors):
            arrays.append(array)
            if array.ndim == 2:
                specs.append(
                    pl.BlockSpec((array.shape[0], 128), lambda i, s, at=at: (0, at(i, s)))
                )
            else:
                specs.append(
                    pl.BlockSpec(
                        (1,) + array.shape[1:], lambda i, s, at=at: (at(i, s), 0, 0)
                    )
                )
    return pl.pallas_call(
        kernel,
        grid_spec=pltpu.PrefetchScalarGridSpec(
            num_scalar_prefetch=1,
            grid=(4,),
            in_specs=specs + [pl.BlockSpec(memory_space=pl.ANY)],
            out_specs=[pl.BlockSpec((1, 384, 384), lambda i, s: (i, 0, 0))] * 2,
        ),
        out_shape=[like(bf16, 4, 384, 384)] * 2,
        compiler_params=params(),
        cost_estimate=cost(1e3, 1e3),
        name="pack_rows",
    )(places, *arrays, mark)


def slot_of(s, step, lead):
    there = s[DPI] ^ step
    x, y = there % 2, there // 2
    return 2 * x + y if lead == XI else 2 * y + x


def unpack(name, places, quarters, pieces, outs):
    columns = quarters[0].shape[2]
    total = 4 * sum(p[1] for p in pieces)

    def kernel(s, *refs):
        scratch = refs[-1]
        for step in range(4):
            for start, rows, lead, base in pieces:
                at = pl.multiple_of(slot_of(s, step, lead) * rows + base, 16)
                scratch[pl.ds(at, rows), :] = refs[step][0, start : start + rows, :].astype(
                    f32
                )
        for out_ref, (_, moves) in zip(refs[4:-1], outs):
            if not moves:
                out_ref[...] = jnp.zeros_like(out_ref)
            for row, rows, to, column in moves:
                out_ref[to : to + rows, column : column + columns] = scratch[
                    row : row + rows, :
                ]

    return pl.pallas_call(
        kernel,
        grid_spec=pltpu.PrefetchScalarGridSpec(
            num_scalar_prefetch=1,
            grid=(1,),
            in_specs=[whole(q) for q in quarters],
            out_specs=[
                pl.BlockSpec(shape, lambda g, s: (0, 0)) for shape, _ in outs
            ],
            scratch_shapes=[pltpu.VMEM((total, columns), f32)],
        ),
        out_shape=[jax.ShapeDtypeStruct(shape, f32) for shape, _ in outs],
        compiler_params=params(),
        cost_estimate=cost(1e3, 1e3),
        name=name,
    )(places, *quarters)


def unpack_mlp(places, quarters):
    def kernel(s, *refs):
        down, up, mark, scratch = refs[8:]
        mark[...] = jnp.zeros_like(mark)
        for pair in range(2):
            for step in range(4):
                block = refs[4 * pair + step]
                for part in range(2):
                    for lead in range(2):
                        at = pl.multiple_of(slot_of(s, step, lead) * 32 + 128 * lead, 32)
                        start = part * 64 + lead * 32
                        scratch[2 * pair + part, pl.ds(at, 32), :] = block[
                            0, start : start + 32, :
                        ].astype(f32)
        for part in range(4):
            down[part * 128 : (part + 1) * 128, :] = scratch[part, :128, :]
            for block in range(8):
                at = (4 * block + part) * 128
                up[:, at : at + 128] = scratch[part, 128:, block * 128 : (block + 1) * 128]

    flat = [q for pair in quarters for q in pair]
    return pl.pallas_call(
        kernel,
        grid_spec=pltpu.PrefetchScalarGridSpec(
            num_scalar_prefetch=1,
            grid=(1,),
            in_specs=[whole(q) for q in flat],
            out_specs=[
                pl.BlockSpec((512, D), lambda g, s: (0, 0)),
                pl.BlockSpec((128, FF), lambda g, s: (0, 0)),
                pl.BlockSpec((8, 128), lambda g, s: (0, 0)),
            ],
            scratch_shapes=[pltpu.VMEM((4, 256, D), f32)],
        ),
        out_shape=[
            jax.ShapeDtypeStruct((512, D), f32),
            jax.ShapeDtypeStruct((128, FF), f32),
            jax.ShapeDtypeStruct((8, 128), f32),
        ],
        compiler_params=params(),
        cost_estimate=cost(1e3, 1e3),
        name="unpack_mlp",
    )(places, *flat)


def ring_rows(places, parts, deps=()):
    def kernel(s, *refs):
        out = refs[-1]
        for k in range(4):
            out[pl.ds(s[ZI] ^ k, 1)] = refs[k][...]

    shape = (4,) + parts[0].shape[1:]
    return pl.pallas_call(
        kernel,
        grid_spec=pltpu.PrefetchScalarGridSpec(
            num_scalar_prefetch=1,
            grid=(1,),
            in_specs=[whole(p) for p in parts]
            + [pl.BlockSpec(memory_space=pl.ANY)] * len(deps),
            out_specs=pl.BlockSpec(shape, lambda g, s: (0, 0, 0)),
        ),
        out_shape=jax.ShapeDtypeStruct(shape, bf16),
        compiler_params=params(),
        cost_estimate=cost(1e3, 1e3),
        name="ring_rows",
    )(places, *parts, *deps)


def stack_rows(places, parts, deps=()):
    _, rows, columns = parts[0].shape
    rows //= 2

    def kernel(s, *refs):
        out = refs[-1]
        for step in range(4):
            for lead in range(2):
                at = pl.multiple_of(slot_of(s, step, lead) * rows + 4 * rows * lead, 16)
                out[:, pl.ds(at, rows), :] = refs[step][:, lead * rows : (lead + 1) * rows, :]

    shape = (4, 8 * rows, columns)
    return pl.pallas_call(
        kernel,
        grid_spec=pltpu.PrefetchScalarGridSpec(
            num_scalar_prefetch=1,
            grid=(1,),
            in_specs=[whole(p) for p in parts]
            + [pl.BlockSpec(memory_space=pl.ANY)] * len(deps),
            out_specs=pl.BlockSpec(shape, lambda g, s: (0, 0, 0)),
        ),
        out_shape=jax.ShapeDtypeStruct(shape, bf16),
        compiler_params=params(),
        cost_estimate=cost(1e3, 1e3),
        name="stack_rows",
    )(places, *parts, *deps)


def last_kernel(
    s, mine, other, norm_cols, unit_cols, weight, weight_rows, unit, inv, gain,
    qkv_out, gain_out, table_out, small_out, by_head,
):
    for z in range(4):
        for q in range(2):
            by_head[2 * z + q] = jnp.where(s[CORE] == q, mine[z], other[z])
    small_out[...] = mine[s[ZI], 256:272, 256:].astype(f32)[:8]
    at = pl.multiple_of(s[SEQI] * 32, 32)
    norm = norm_cols[...]
    cols_grad = jnp.zeros((VOCAB, 128), f32)
    normed_grad = jnp.zeros((32, D), f32)
    for h in range(HEADS):
        for t in range(3):
            lanes = slice(t * 128, (t + 1) * 128)
            to = slice(t * D + h * 128, t * D + (h + 1) * 128)
            g = by_head[h, :VOCAB, lanes]
            qkv_out[:, to] = dot(norm, g, TN)
            cols_grad = cols_grad + dot(g, weight_rows[:, to], NT)
            normed_grad = normed_grad + dot(
                by_head[h, pl.ds(at, 32), lanes], weight[:, to], NT
            )
    gain_out[...] = jnp.sum(cols_grad * unit_cols[...], axis=0, keepdims=True)
    u = unit[...]
    scaled = normed_grad * gain[...]
    a = jnp.mean(scaled, axis=-1, keepdims=True)
    b = jnp.mean(scaled * u, axis=-1, keepdims=True)
    low = pl.multiple_of(VOCAB + (s[SEQI] % 4) * 32, 32)
    rows_sum = [
        jnp.where(
            s[SEQI] < 4,
            by_head[h, pl.ds(low, 32), :128].astype(f32),
            by_head[h, pl.ds(low, 32), 128:256].astype(f32),
        )
        for h in range(HEADS)
    ]
    table_out[...] = (
        jnp.concatenate(rows_sum, axis=1) + (scaled - a - u * b) * inv[:, :1]
    )


def last_products(places, mine, other, normed, unit, weight, inv, gain):
    return pl.pallas_call(
        last_kernel,
        grid_spec=pltpu.PrefetchScalarGridSpec(
            num_scalar_prefetch=1,
            grid=(1,),
            in_specs=[
                whole(mine),
                whole(other),
                pl.BlockSpec((VOCAB, 128), lambda g, s: (0, s[SEQI])),
                pl.BlockSpec((VOCAB, 128), lambda g, s: (0, s[SEQI])),
                whole(weight),
                pl.BlockSpec((128, 3 * D), lambda g, s: (s[SEQI], 0)),
                pl.BlockSpec((32, D), lambda g, s: (s[SEQI], 0)),
                pl.BlockSpec((32, 128), lambda g, s: (s[SEQI], 0)),
                whole(gain),
            ],
            out_specs=[
                pl.BlockSpec((128, 3 * D), lambda g, s: (0, 0)),
                pl.BlockSpec((1, 128), lambda g, s: (0, 0)),
                pl.BlockSpec((32, D), lambda g, s: (0, 0)),
                pl.BlockSpec((8, 128), lambda g, s: (0, 0)),
            ],
            scratch_shapes=[pltpu.VMEM((HEADS, 384, 384), bf16)],
        ),
        out_shape=[
            jax.ShapeDtypeStruct((128, 3 * D), f32),
            jax.ShapeDtypeStruct((1, 128), f32),
            jax.ShapeDtypeStruct((32, D), f32),
            jax.ShapeDtypeStruct((8, 128), f32),
        ],
        compiler_params=params(),
        cost_estimate=cost(1e3, 1e3),
        name="last_products",
    )(places, mine, other, normed, unit, weight, weight, unit, inv, gain)


def total_of(value):
    flat = value.reshape((-1,) + value.shape[2:])
    own = lax.psum_scatter(flat, "seq", scatter_dimension=0, tiled=True)
    return lax.psum(own, "dp").astype(f32)


def places_of():
    here = lax.axis_index("seq")
    dp = lax.axis_index("dp")
    return jnp.stack([dp % 2, dp // 2, here // 2, here % 2, dp, here]).astype(jnp.int32)


def prepare_kernel(
    places, blocks_a, blocks_b, gate, bias, picks, mask, *rest
):
    span, live, counts, rows, pick, pick_t, forget, bias_out = rest[-8:]
    here = places[SEQI]
    sign = lax.broadcasted_iota(jnp.int32, (VOCAB, 128), 0)
    first = jnp.zeros((1, 128), f32)
    before = jnp.zeros((4, 128), jnp.int32)
    for k in range(8):
        block = blocks_a[k] if k < 4 else blocks_b[k - 4]
        w = here ^ k
        total = jnp.zeros((VOCAB, 128), f32)
        for r in range(4):
            total = total + jnp.where(block[r : r + 1] == sign, 1.0, 0.0)
        count = jnp.broadcast_to(jnp.sum(total, axis=1, keepdims=True), (VOCAB, 128))
        counts[pl.ds(w, 1)] = count[None]
        rows[pl.ds(w, 1)] = count.T[:1][None]
        marked = jnp.where(block[4:5] > 0, w.astype(f32), 0.0)
        first = jnp.maximum(first, jnp.where(w <= here, marked, 0.0))
        before = jnp.where(w == here - 1, block[:4], before)
    span[0] = jnp.max(first).astype(jnp.int32)
    span[1] = here
    live[0] = 1 - jnp.max(blocks_a[0, 4:5].astype(f32)).astype(jnp.int32)
    own = blocks_a[0, :4]
    for r in range(8):
        ids = before[r : r + 1] if r < 4 else own[r - 4 : r - 3]
        one = jnp.where(ids == sign, 1.0, 0.0)
        pick_t[:, r * 128 : (r + 1) * 128] = one.astype(bf16)
        pick[r * 128 : (r + 1) * 128, :] = one.T.astype(bf16)
    forget[...] = 1.0 / (1.0 + jnp.exp(-gate[...]))
    table = lax.dot_general(
        bias[...], picks[...], NN, precision=lax.Precision.HIGHEST, preferred_element_type=f32
    )
    table = table * log2e + mask[...]
    for h in range(HEADS):
        bias_out[h] = table[h : h + 1]


def prepare(places, char_ids, seg_starts, gate_logit, distance_bias, deps=()):
    packed = jnp.concatenate(
        [
            char_ids.reshape(4, 128),
            jnp.broadcast_to(seg_starts, (1, 128)),
            jnp.zeros((3, 128), jnp.int32),
        ],
        axis=0,
    )[None]
    for bit in (1, 2):
        packed = jnp.concatenate(
            [packed, permute(packed, "seq", lambda i, bit=bit: i ^ bit)], axis=0
        )
    beyond = permute(packed, "seq", lambda i: i ^ 4)
    ins = (
        packed,
        beyond,
        gate_logit.reshape(1, D),
        distance_bias.reshape(HEADS, BUCKETS),
        jnp.asarray(lane_pick()),
        jnp.asarray(lane_hidden()),
    )
    outs = (
        like(jnp.int32, 2),
        like(jnp.int32, 1),
        like(f32, 8, VOCAB, 128),
        like(f32, 8, 1, VOCAB),
        like(bf16, CONTEXT, VOCAB),
        like(bf16, VOCAB, CONTEXT),
        like(f32, 1, D),
        like(f32, HEADS, 1, CONTEXT),
    )
    return pl.pallas_call(
        prepare_kernel,
        grid_spec=pltpu.PrefetchScalarGridSpec(
            num_scalar_prefetch=1,
            grid=(1,),
            in_specs=[whole(a) for a in ins]
            + [pl.BlockSpec(memory_space=pl.ANY)] * len(deps),
            out_specs=[pl.BlockSpec(memory_space=pltpu.SMEM)] * 2
            + [whole(o) for o in outs[2:]],
        ),
        out_shape=list(outs),
        compiler_params=params(),
        cost_estimate=cost(1e3, 1e3),
        name="prepare",
    )(places, *ins, *deps)


def plain_prepare(char_ids, seg_starts, gate_logit, distance_bias):
    windows = lax.axis_size("seq")
    here = lax.axis_index("seq")
    packed = jnp.concatenate(
        [char_ids.reshape(4, 128), jnp.broadcast_to(seg_starts, (1, 128))], axis=0
    )
    everyone = lax.all_gather(packed, "seq")
    ids_all = everyone[:, :4].reshape(windows, WINDOW)
    flags = everyone[:, 4, 0]
    order = jnp.arange(windows, dtype=jnp.int32)
    first = jnp.max(jnp.where((flags > 0) & (order <= here), order, 0))
    span = jnp.stack([first, here]).astype(jnp.int32)
    live = (1 - seg_starts.reshape(1)).astype(jnp.int32)
    vocab = jnp.arange(VOCAB, dtype=jnp.int32)
    counts = jnp.sum(
        (ids_all[:, :, None] == vocab[None, None, :]).astype(f32), axis=1
    )
    before = lax.dynamic_index_in_dim(ids_all, jnp.maximum(here - 1, 0), 0, False)
    context_ids = jnp.concatenate([before, char_ids.reshape(-1)])
    bias_rows = jnp.dot(
        distance_bias.reshape(HEADS, BUCKETS),
        jnp.asarray(lane_pick()),
        precision=lax.Precision.HIGHEST,
    ) * log2e + jnp.asarray(lane_hidden())
    return (
        span,
        live,
        jnp.broadcast_to(counts[:, :, None], (windows, VOCAB, 128)),
        counts[:, None, :],
        (context_ids[:, None] == vocab[None, :]).astype(bf16),
        (vocab[:, None] == context_ids[None, :]).astype(bf16),
        jax.nn.sigmoid(gate_logit).reshape(1, D),
        bias_rows.reshape(HEADS, 1, CONTEXT),
    )


def body(
    char_ids,
    seg_starts,
    char_table,
    norm_gain,
    qkv_weight,
    distance_bias,
    state_query,
    state_init,
    state_gain,
    state_kv_weight,
    gate_logit,
    out_weight,
    mlp_gain,
    up_weight,
    down_weight,
    cotangent,
):
    windows = lax.axis_size("seq")
    here = lax.axis_index("seq")
    norm_gain, state_gain, mlp_gain = (
        t.reshape(1, D) for t in (norm_gain, state_gain, mlp_gain)
    )
    table_unit, table_inv, normed_table, qkv_table = table_forward(
        char_table, norm_gain, qkv_weight
    )

    characters = (char_ids, seg_starts, gate_logit, distance_bias)
    if fitted():
        places = places_of()
        prepared = prepare(places, *characters, (qkv_table,))
    else:
        prepared = plain_prepare(*characters)
    span, live, counts, count_rows, pick, pick_t, forget, bias_rows = prepared
    states_in, forget_slope, lowest = summary_forward(
        span, state_query, qkv_table, counts, count_rows, state_init, forget
    )
    state_unit, state_inv, state_normed, state_kv = states_forward(
        states_in, state_gain, state_kv_weight
    )
    mixed, lse = attention_forward(
        live, pick, pick_t, qkv_table, state_kv, state_kv, bias_rows
    )
    residual, mlp_unit, mlp_inv, mlp_in, mlp_split = residual_forward(
        places if fitted() else jnp.zeros(6, jnp.int32),
        mixed,
        out_weight,
        pick,
        char_table,
        mlp_gain,
    )
    upstream = cotangent.reshape(WINDOW, D)

    close_up = fitted_tail if fitted() else plain_tail
    return close_up(dict(locals()))


def fitted_tail(values):
    v = types.SimpleNamespace(**values)
    places = v.places
    weights = (v.upstream, v.up_weight, v.down_weight)

    out, gx = v.residual, jnp.zeros((WINDOW, D), f32)
    traffic = Traffic(places)
    parts, deps = [], ()
    for part in range(4):
        send, keep, out, gx = mlp_packed(
            part, places, v.mlp_in, v.mlp_split, *weights, out, gx, deps
        )
        if part:
            second = parts[part - 2] if part > 1 else ()
            mark = traffic.boundary((gx,), parts[part - 1], second, swap=[send])
            deps = (mark,)
            came = traffic.swapped[0]
        else:
            came = traffic.swap(send)
        parts.append(wings(keep, came))
    layer_out = out.astype(bf16).reshape(1, WINDOW, D)
    front = Column(parts[0] + parts[1])
    back = Column(parts[2] + parts[3])

    grad_mlp_gain, grad_out, grad_mixed, rows_sum = feed_back(v, gx, (mark,))
    gsk, gsv, gq, inner = state_backward(
        v.pick, v.qkv_table, v.state_kv, v.lse, v.mixed, grad_mixed
    )
    mark = traffic.boundary((inner,), parts[3], parts[2], near=[front])
    grad_k, grad_v, grad_state_gain, local, grad_gate = states_back(v, gsk, gsv, (mark,))
    send, keep = packed_pair(
        "pack_middle",
        places,
        [t.reshape(8, 128, D) for t in (grad_k, grad_v, grad_out)],
    )
    middle = wings(keep, traffic.swap(send))
    summary_args = (
        v.span, v.state_query, v.qkv_table, v.counts, v.count_rows, local, v.forget, v.lowest
    )
    onto = summary_backward(*summary_args, (send,), 0)
    mark = traffic.boundary((onto[0],), middle, parts[3], far=[front])
    g, gsq, ginit = summary_backward(*summary_args, (mark,), 1, onto)
    mark = traffic.boundary((g,), (), middle, near=[back], close=[front])
    send, keep = packed_pair(
        "pack_states", places, [gsq.reshape(8, 64, D), ginit.reshape(8, 64, D)], (mark,)
    )
    states = wings(keep, traffic.swap(send))
    tokens_args = (
        v.live, v.pick, v.pick_t, v.qkv_table, v.bias_rows, v.lse, inner, grad_mixed, gq
    )
    onto = token_backward(*tokens_args, (send,), 0)
    mark = traffic.boundary((onto[1],), states, far=[back])
    front_rows = traffic.spread(front.own)
    g_tokens, fold = token_backward(*tokens_args, (mark,), 1, onto)
    side, rest = Column(middle), Column(states)
    mark = traffic.boundary((fold,), (), states, near=[side], close=[back])
    send, keep = pack_rows(
        places, mark, g_tokens, g, rows_sum, grad_mlp_gain, grad_state_gain, grad_gate, fold
    )
    rows = wings(keep, traffic.swap(send))
    last = Column(rows)
    traffic.boundary((), rows, near=[rest], far=[side])
    traffic.boundary((), (), rows, far=[rest])
    back_rows = traffic.spread(back.own, 2)
    traffic.boundary((), near=[last], join=[side, rest])
    side_own = traffic.joined
    traffic.boundary((), far=[last])
    side_rows = traffic.spread(side_own)
    grad_down, grad_up, mark = unpack_mlp(places, [front_rows, back_rows])
    traffic.boundary((mark,), close=[last])
    beside = permute(last.own, "seq", lambda i: i ^ 2)
    row_ring = [
        last.own,
        beside,
        permute(last.own, "seq", lambda i: i ^ 4),
        permute(beside, "seq", lambda i: i ^ 4),
    ]
    ring = ring_rows(places, row_ring)
    ring_parts = traffic.spread(ring)
    grad_state_kv, grad_out, grad_state_query, grad_state_init, mark = unpack(
        "unpack_side",
        places,
        side_rows,
        [(0, 48, XI, 0), (48, 48, YI, 192), (96, 16, XI, 384), (112, 16, YI, 448)],
        [
            ((128, 2 * D), [(0, 128, 0, 0), (128, 128, 0, D)]),
            ((128, D), [(256, 128, 0, 0)]),
            ((64, D), [(384, 64, 0, 0)]),
            ((64, D), [(448, 64, 0, 0)]),
            ((8, 128), []),
        ],
    )
    mine = stack_rows(places, ring_parts, (mark,))
    other = swap_core(mine)
    grad_qkv, grad_norm_gain, grad_table, small = last_products(
        places,
        mine,
        other,
        v.normed_table,
        v.table_unit,
        v.qkv_weight,
        v.table_inv,
        v.norm_gain,
    )
    return (
        layer_out,
        grad_table,
        grad_norm_gain.reshape(-1),
        grad_qkv,
        small[3, :32],
        grad_state_query,
        grad_state_init,
        small[1],
        grad_state_kv,
        small[2],
        grad_out,
        small[0],
        grad_up,
        grad_down,
    )


def plain_tail(values):
    v = types.SimpleNamespace(**values)
    windows, here = v.windows, v.here
    shard = lambda n: n // windows
    out, gx = v.residual, jnp.zeros((WINDOW, D), f32)
    grads_down, grads_up = [], []
    for part in range(SPLITS):
        gd, gu, out, gx = mlp_part(
            part, v.mlp_in, v.upstream, v.up_weight, v.down_weight, out, gx
        )
        grads_down.append(gd)
        grads_up.append(gu)
    layer_out = out.astype(bf16).reshape(1, WINDOW, D)
    grad_mlp_gain, grad_out, grad_mixed, rows_sum = feed_back(v, gx)
    gsk, gsv, gq, inner = state_backward(
        v.pick, v.qkv_table, v.state_kv, v.lse, v.mixed, grad_mixed
    )
    grad_k, grad_v, grad_state_gain, local, grad_gate = states_back(v, gsk, gsv)
    g, gsq, ginit = summary_backward(
        v.span, v.state_query, v.qkv_table, v.counts, v.count_rows, local, v.forget,
        v.lowest,
    )
    g_tokens, fold = token_backward(
        v.live, v.pick, v.pick_t, v.qkv_table, v.bias_rows, v.lse, inner, grad_mixed, gq
    )
    g = (g.astype(f32) + g_tokens).astype(bf16)
    sharded = lambda t: total_of(t.reshape(windows, -1, t.shape[-1]))
    full = jnp.stack([t.reshape(-1, TILE, D) for t in grads_down], axis=1)
    grad_down = sharded(full.reshape(FF, D))
    full = jnp.stack([t.reshape(D, -1, TILE) for t in grads_up], axis=2)
    grad_up = sharded(full.reshape(D, FF))
    grad_state_kv = sharded(jnp.concatenate([grad_k, grad_v], axis=1))
    small = jnp.concatenate(
        [
            t.reshape(windows, -1)
            for t in (grad_mlp_gain, grad_state_gain, grad_gate, fold[:, 0, :BUCKETS])
        ],
        axis=1,
    )
    small = total_of(small[:, None, :])[0]
    cut = shard(D)
    all_rows = lax.psum(g, ("dp", "seq"))
    grad_rows = jnp.concatenate(
        [
            all_rows[:, :, t * 128 : (t + 1) * 128].transpose(1, 0, 2).reshape(VOCAB, D)
            for t in range(3)
        ],
        axis=1,
    )
    mine = lax.dynamic_slice_in_dim(v.normed_table, here * cut, cut, 1)
    weight_rows = lax.dynamic_slice_in_dim(v.qkv_weight, here * cut, cut, 0)
    unit_cols = lax.dynamic_slice_in_dim(v.table_unit, here * cut, cut, 1)
    at = here * shard(VOCAB)
    take = lambda t: lax.dynamic_slice_in_dim(t, at, shard(VOCAB), 0)
    grad_table = sharded(rows_sum) + norm_back(
        take(v.table_unit),
        take(v.table_inv)[:, :1],
        v.norm_gain,
        dot(take(grad_rows), v.qkv_weight, NT),
    )
    return (
        layer_out,
        grad_table,
        jnp.sum(dot(grad_rows, weight_rows, NT) * unit_cols, axis=0),
        dot(mine, grad_rows, TN),
        small[3 * cut :],
        sharded(gsq),
        sharded(ginit),
        small[cut : 2 * cut],
        grad_state_kv,
        small[2 * cut : 3 * cut],
        sharded(grad_out),
        small[:cut],
        grad_up,
        grad_down,
    )


def solution(mesh):
    placed = (P("dp", "seq"), P("dp", "seq")) + (P(),) * 13 + (P("dp", "seq", None),)
    return jax.shard_map(
        body,
        mesh=mesh,
        in_specs=placed,
        out_specs=(
            P("dp", "seq", None),
            P("seq", None),
            P("seq"),
            P("seq", None),
            P("seq"),
            P("seq", None),
            P("seq", None),
            P("seq"),
            P("seq", None),
            P("seq"),
            P("seq", None),
            P("seq"),
            P("seq", None),
            P("seq", None),
        ),
        check_vma=False,
    )
```

profile of v0, /device:TPU:0, one launch (start us, length us, event | category | flops | bytes accessed | tf_op | source)
XLA Modules:
  0.0 341.5 jit_solution(11788447988619513931)
XLA Ops:
  11.8 7.0 %table_forward.1 = (f32[256,1024]{1,0:T(8,128)}, f32[256,128]{1,0:T(8,128)}, bf16[256,1024]{1,0:T(8,128)(2,1)}, bf16[256,3072]{1,0:T(8,128)(2,1)S(1)}) custom-call(bf16[256,1024]{1,0:T(8,128)(2,1)} %table.3, f32[1,1024]{1,0:T(1,128)S(1)} %bitcast.55, bf16[1024,3072]{1,0:T(8,128)(2,1)} %weight_rows.1), custom_call_target="tpu_custom_call" | custom-call | flops 1000 | bytes 1000 | tf_op jit(solution)/shard_map/table_forward/pallas_call | solution.py:828
  21.1 6.2 %summary_forward.1 = (f32[512,1024]{1,0:T(8,128)S(1)}, f32[512,1024]{1,0:T(8,128)}, f32[2,8,128]{2,1,0:T(8,128)S(1)}) custom-call(s32[2]{0:T(128)S(1)} %get-tuple-element.141.span, bf16[512,1024]{1,0:T(8,128)(2,1)S(1)} %copy-done.32, bf16[256,3072]{1,0:T(8,128)(2,1)S(1)} %get-tuple-element.137.rest_0_.kt.vt.refs_3_.refs_4_.refs_5_.refs_1_, ...), custom_call_target="tpu_custom_call" | custom-call | flops 1000 | bytes 1000 | tf_op jit(solution)/shard_map/summary_forward/pallas_call | solution.py:195
  27.3 4.9 %states_forward.1 = (f32[512,1024]{1,0:T(8,128)}, f32[512,128]{1,0:T(8,128)}, bf16[512,1024]{1,0:T(8,128)(2,1)}, bf16[512,2048]{1,0:T(8,128)(2,1)S(1)}) custom-call(f32[512,1024]{1,0:T(8,128)S(1)} %get-tuple-element.145.states, f32[1,1024]{1,0:T(1,128)S(1)} %bitcast.53, bf16[1024,2048]{1,0:T(8,128)(2,1)S(1)} %copy-done.25), custom_call_target="tpu_custom_call" | custom-call | flops 1000 | bytes 1000 | tf_op jit(solution)/shard_map/states_forward/pallas_call | solution.py:869
  32.2 15.4 %attention_forward.1 = (bf16[512,1024]{1,0:T(8,128)(2,1)S(1)}, f32[8,1,512]{2,1,0:T(1,128)S(1)}) custom-call(s32[1]{0:T(128)} %get-tuple-element.138.refs_0_, bf16[1024,256]{1,0:T(8,128)(2,1)S(1)} %get-tuple-element.139.refs_1_.pick.refs_0_, bf16[256,1024]{1,0:T(8,128)(2,1)S(1)} %get-tuple-element.140.refs_2_, ...), custom_call_target="tpu_custom_call" | custom-call | flops 1000 | bytes 1000 | tf_op jit(solution)/shard_map/attention_forward/pallas_call | solution.py:410
  53.8 10.1 %feed_forward.4 = (bf16[4,256,1024]{2,1,0:T(8,128)(2,1)S(1)}, bf16[4,256,1024]{2,1,0:T(8,128)(2,1)S(1)}, f32[512,1024]{1,0:T(8,128)S(1)}, f32[512,1024]{1,0:T(8,128)S(1)}) custom-call(s32[6]{0:T(128)S(1)} %stack.27.places.s, bf16[512,1024]{1,0:T(8,128)(2,1)S(1)} %get-tuple-element.149.x, bf16[2,512,512]{2,1,0:T(8,128)(2,1)S(1)} %get-tuple-element.150.xs, ...), custom_call_target="tpu_custom_call" | custom-call | flops 1000 | bytes 1000 | tf_op jit(solution)/shard_map/feed_forward/pallas_call | solution.py:746
  64.0 10.3 %feed_forward.5 = (bf16[4,256,1024]{2,1,0:T(8,128)(2,1)S(1)}, bf16[4,256,1024]{2,1,0:T(8,128)(2,1)S(1)}, f32[512,1024]{1,0:T(8,128)S(1)}, f32[512,1024]{1,0:T(8,128)S(1)}) custom-call(s32[6]{0:T(128)S(1)} %stack.27.places.s, bf16[512,1024]{1,0:T(8,128)(2,1)S(1)} %get-tuple-element.149.x, bf16[2,512,512]{2,1,0:T(8,128)(2,1)S(1)} %get-tuple-element.150.xs, ...), custom_call_target="tpu_custom_call" | custom-call | flops 1000 | bytes 1000 | tf_op jit(solution)/shard_map/feed_forward/pallas_call | solution.py:746
  78.8 11.1 %feed_forward.6 = (bf16[4,256,1024]{2,1,0:T(8,128)(2,1)}, bf16[4,256,1024]{2,1,0:T(8,128)(2,1)S(1)}, f32[512,1024]{1,0:T(8,128)S(1)}, f32[512,1024]{1,0:T(8,128)S(1)}) custom-call(s32[6]{0:T(128)S(1)} %stack.27.places.s, bf16[512,1024]{1,0:T(8,128)(2,1)S(1)} %get-tuple-element.149.x, bf16[2,512,512]{2,1,0:T(8,128)(2,1)S(1)} %get-tuple-element.150.xs, ...), custom_call_target="tpu_custom_call" | custom-call | flops 1000 | bytes 1000 | tf_op jit(solution)/shard_map/feed_forward/pallas_call | solution.py:746
  99.4 11.1 %feed_forward.7 = (bf16[4,256,1024]{2,1,0:T(8,128)(2,1)}, bf16[4,256,1024]{2,1,0:T(8,128)(2,1)S(1)}, f32[512,1024]{1,0:T(8,128)S(1)}, f32[512,1024]{1,0:T(8,128)S(1)}) custom-call(s32[6]{0:T(128)S(1)} %stack.27.places.s, bf16[512,1024]{1,0:T(8,128)(2,1)S(1)} %copy-done.22, bf16[2,512,512]{2,1,0:T(8,128)(2,1)S(1)} %copy-done.24, ...), custom_call_target="tpu_custom_call" | custom-call | flops 1000 | bytes 1000 | tf_op jit(solution)/shard_map/feed_forward/pallas_call | solution.py:746
  128.1 10.8 %state_backward.1 = (bf16[512,1024]{1,0:T(8,128)(2,1)}, bf16[512,1024]{1,0:T(8,128)(2,1)}, f32[8,128,512]{2,1,0:T(8,128)S(1)}, f32[8,1,512]{2,1,0:T(1,128)S(1)}) custom-call(bf16[1024,256]{1,0:T(8,128)(2,1)S(1)} %copy-done.19, bf16[256,3072]{1,0:T(8,128)(2,1)S(1)} %get-tuple-element.137.rest_0_.kt.vt.refs_3_.refs_4_.refs_5_.refs_1_, ...), custom_call_target="tpu_custom_call" | custom-call | flops 1000 | bytes 1000 | tf_op jit(solution)/shard_map/state_backward/pallas_call | solution.py:484
  143.2 10.1 %states_back.1 = (bf16[1024,1024]{1,0:T(8,128)(2,1)S(1)}, bf16[1024,1024]{1,0:T(8,128)(2,1)S(1)}, f32[1,1024]{1,0:T(1,128)S(1)}, f32[512,1024]{1,0:T(8,128)S(1)}, f32[1,1024]{1,0:T(1,128)S(1)}) custom-call(bf16[512,1024]{1,0:T(8,128)(2,1)} %get-tuple-element.180.gsk, bf16[512,1024]{1,0:T(8,128)(2,1)} %get-tuple-element.181.gsv, bf16[1024,2048]{1,0:T(8,128)(2,1)} %weight.6, ...), custom_call_target="tpu_custom_call" | custom-call | flops 1000 | bytes 1000 | tf_op jit(solution)/shard_map/states_back/pallas_call | solution.py:782
  162.5 8.8 %collective-permute-done.16.refs_11_.refs_15_.refs_39_ = bf16[2,128,1024]{2,1,0:T(8,128)(2,1)S(1)} collective-permute-done((bf16[2,128,1024]{2,1,0:T(8,128)(2,1)S(1)}, bf16[2,128,1024]{2,1,0:T(8,128)(2,1)S(1)}, u32[]{:S(2)}, u32[]{:S(2)}) %collective-permute-start.16) | collective-permute-done | bytes 524320 | tf_op jit(solution)/shard_map/ppermute | solution.py:1011
  187.0 6.6 %collective-permute-done.19.refs_40_.refs_44_ = bf16[1,128,1024]{2,1,0:T(8,128)(2,1)S(1)} collective-permute-done((bf16[1,128,1024]{2,1,0:T(8,128)(2,1)S(1)}, bf16[1,128,1024]{2,1,0:T(8,128)(2,1)S(1)}, u32[]{:S(2)}, u32[]{:S(2)}) %collective-permute-start.19) | collective-permute-done | bytes 262176 | tf_op jit(solution)/shard_map/ppermute | solution.py:1011
  193.7 7.3 %collective-permute-done.17.refs_2_.refs_17_.refs_33_.refs_43_.refs_12_.refs_20_ = bf16[4,128,1024]{2,1,0:T(8,128)(2,1)S(1)} collective-permute-done((bf16[4,128,1024]{2,1,0:T(8,128)(2,1)S(1)}, bf16[4,128,1024]{2,1,0:T(8,128)(2,1)S(1)}, u32[]{:S(2)}, u32[]{:S(2)}) %collective-permute-start.17) | collective-permute-done | bytes 1048608 | tf_op jit(solution)/shard_map/ppermute | solution.py:1011
  211.4 12.0 %token_backward.2 = (f32[8,256,384]{2,1,0:T(8,128)S(1)}, f32[8,1,128]{2,1,0:T(1,128)S(1)}) custom-call(s32[1]{0:T(128)} %get-tuple-element.138.refs_0_, bf16[1024,256]{1,0:T(8,128)(2,1)S(1)} %copy-done.20, bf16[256,1024]{1,0:T(8,128)(2,1)S(1)} %copy-done.53, bf16[256,3072]{1,0:T(8,128)(2,1)S(1)} %get-tuple-element.137.rest_0_.kt.vt.refs_3_.refs_4_.refs_5_.refs_1_, ...), custom_call_target="tpu_custom_call" | custom-call | flops 1000 | bytes 1000 | tf_op jit(solution)/shard_map/token_backward/pallas_call | solution.py:594
  234.3 12.0 %token_backward.3 = (f32[8,256,384]{2,1,0:T(8,128)S(1)}, f32[8,1,128]{2,1,0:T(1,128)S(1)}) custom-call(s32[1]{0:T(128)} %get-tuple-element.138.refs_0_, bf16[1024,256]{1,0:T(8,128)(2,1)S(1)} %copy-done.20, bf16[256,1024]{1,0:T(8,128)(2,1)S(1)} %copy-done.53, ...), custom_call_target="tpu_custom_call", output_to_operand_aliasing={{0}: (13, {}), {1}: (14, {})} | custom-call | flops 1000 | bytes 1000 | tf_op jit(solution)/shard_map/token_backward/pallas_call | solution.py:594
  255.9 4.9 %collective-permute-done.33.refs_21_.refs_24_.refs_17_ = bf16[2,96,1024]{2,1,0:T(8,128)(2,1)S(1)} collective-permute-done((bf16[2,96,1024]{2,1,0:T(8,128)(2,1)S(1)}, bf16[2,96,1024]{2,1,0:T(8,128)(2,1)S(1)}, u32[]{:S(2)}, u32[]{:S(2)}) %collective-permute-start.33) | collective-permute-done | bytes 393248 | tf_op jit(solution)/shard_map/ppermute | solution.py:1011
  266.6 4.7 %collective-permute-done.36.refs_7_.refs_10_.refs_20_ = bf16[2,32,1024]{2,1,0:T(8,128)(2,1)S(1)} collective-permute-done((bf16[2,32,1024]{2,1,0:T(8,128)(2,1)S(1)}, bf16[2,32,1024]{2,1,0:T(8,128)(2,1)S(1)}, u32[]{:S(2)}, u32[]{:S(2)}) %collective-permute-start.36) | collective-permute-done | bytes 131104 | tf_op jit(solution)/shard_map/ppermute | solution.py:1011
  278.2 4.9 %collective-permute-done.43.refs_27_.refs_7_ = bf16[1,128,1024]{2,1,0:T(8,128)(2,1)S(1)} collective-permute-done((bf16[1,128,1024]{2,1,0:T(8,128)(2,1)S(1)}, bf16[1,128,1024]{2,1,0:T(8,128)(2,1)S(1)}, u32[]{:S(2)}, u32[]{:S(2)}) %collective-permute-start.43) | collective-permute-done | bytes 262176 | tf_op jit(solution)/shard_map/ppermute | solution.py:1011
  287.5 5.6 %collective-permute-done.46.refs_5_.refs_1_ = bf16[1,128,1024]{2,1,0:T(8,128)(2,1)S(1)} collective-permute-done((bf16[1,128,1024]{2,1,0:T(8,128)(2,1)S(1)}, bf16[1,128,1024]{2,1,0:T(8,128)(2,1)S(1)}, u32[]{:S(2)}, u32[]{:S(2)}) %collective-permute-start.46) | collective-permute-done | bytes 262176 | tf_op jit(solution)/shard_map/ppermute | solution.py:1011
  294.2 4.9 %collective-permute-done.44.refs_1_.refs_2_ = bf16[2,96,384]{2,1,0:T(8,128)(2,1)S(1)} collective-permute-done((bf16[2,96,384]{2,1,0:T(8,128)(2,1)S(1)}, bf16[2,96,384]{2,1,0:T(8,128)(2,1)S(1)}, u32[]{:S(2)}, u32[]{:S(2)}) %collective-permute-start.44) | collective-permute-done | bytes 147488 | tf_op jit(solution)/shard_map/ppermute | solution.py:1011
  312.6 5.1 %collective-permute-done.51.refs_3_ = bf16[1,96,384]{2,1,0:T(8,128)(2,1)S(1)} collective-permute-done((bf16[1,96,384]{2,1,0:T(8,128)(2,1)S(1)}, bf16[1,96,384]{2,1,0:T(8,128)(2,1)S(1)}, u32[]{:S(2)}, u32[]{:S(2)}) %collective-permute-start.51) | collective-permute-done | bytes 73760 | tf_op jit(solution)/shard_map/ppermute | solution.py:1011
  320.1 5.0 %collective-permute-done.52.refs_1_ = bf16[4,96,384]{2,1,0:T(8,128)(2,1)S(1)} collective-permute-done((bf16[4,96,384]{2,1,0:T(8,128)(2,1)S(1)}, bf16[4,96,384]{2,1,0:T(8,128)(2,1)S(1)}, u32[]{:S(2)}, u32[]{:S(2)}) %collective-permute-start.52) | collective-permute-done | bytes 294944 | tf_op jit(solution)/shard_map/ppermute | solution.py:1011
  327.3 4.5 %collective-permute-done.54.refs_3_ = bf16[4,96,384]{2,1,0:T(8,128)(2,1)S(1)} collective-permute-done((bf16[4,96,384]{2,1,0:T(8,128)(2,1)S(1)}, bf16[4,96,384]{2,1,0:T(8,128)(2,1)S(1)}, u32[]{:S(2)}, u32[]{:S(2)}) %collective-permute-start.54) | collective-permute-done | bytes 294944 | tf_op jit(solution)/shard_map/ppermute | solution.py:1011
  335.5 4.7 %last_products.1 = (f32[128,3072]{1,0:T(8,128)}, f32[1,128]{1,0:T(1,128)}, f32[32,1024]{1,0:T(8,128)}, f32[8,128]{1,0:T(8,128)S(1)}) custom-call(s32[6]{0:T(128)S(1)} %stack.27.places.s, bf16[4,384,384]{2,1,0:T(8,128)(2,1)S(1)} %stack_rows.1.mine, bf16[4,384,384]{2,1,0:T(8,128)(2,1)S(1)} %collective-permute-done.55.other, bf16[256,1024]{1,0:T(8,128)(2,1)S(1)} %copy-done.68, ...), custom_call_target="tpu_custom_call" | custom-call | flops 1000 | bytes 1000 | tf_op jit(solution)/shard_map/last_products/pallas_call | solution.py:1481
  (305 shorter events, 150.5 us)
Async XLA Ops:
  75.2 15.7 %collective-permute-start.4 = (bf16[4,256,1024]{2,1,0:T(8,128)(2,1)S(1)}, bf16[4,256,1024]{2,1,0:T(8,128)(2,1)S(1)}, u32[]{:S(2)}, u32[]{:S(2)}) collective-permute-start(bf16[4,256,1024]{2,1,0:T(8,128)(2,1)S(1)} %get-tuple-element.163), channel_id=1, source_target_pairs={{0,1},{1,0},{2,3},{3,2},{4,5},{5,4},{6,7},{7,6},{8,9},{9,8},{10,11... | collective-permute-start | bytes 6291464 | tf_op jit(solution)/shard_map/ppermute | solution.py:1011
  92.2 21.0 %collective-permute-start.7 = (bf16[4,256,1024]{2,1,0:T(8,128)(2,1)}, bf16[4,256,1024]{2,1,0:T(8,128)(2,1)S(1)}, u32[]{:S(2)}, u32[]{:S(2)}) collective-permute-start(bf16[4,256,1024]{2,1,0:T(8,128)(2,1)} %get-tuple-element.173), channel_id=1, source_target_pairs={{0,1},{1,0},{2,3},{3,2},{4,5},{5,4},{6,7},{7,6},{8,9},{9,8},{10,11... | collective-permute-start | bytes 6291464 | tf_op jit(solution)/shard_map/ppermute | solution.py:1011
  92.2 21.0 %collective-permute-start.8 = (bf16[4,96,1024]{2,1,0:T(8,128)(2,1)S(1)}, bf16[4,96,1024]{2,1,0:T(8,128)(2,1)S(1)}, u32[]{:S(2)}, u32[]{:S(2)}) collective-permute-start(bf16[4,96,1024]{2,1,0:T(8,128)(2,1)S(1)} %get-tuple-element.174), channel_id=1, source_target_pairs={{0,16},{8,24},{16,0},{24,8},{1,17},{9,25},{17,1},{25,9},{2,18},{10... | collective-permute-start | bytes 2359304 | tf_op jit(solution)/shard_map/ppermute | solution.py:1011
  92.7 20.5 %collective-permute-start.9 = (bf16[4,96,1024]{2,1,0:T(8,128)(2,1)S(1)}, bf16[4,96,1024]{2,1,0:T(8,128)(2,1)S(1)}, u32[]{:S(2)}, u32[]{:S(2)}) collective-permute-start(bf16[4,96,1024]{2,1,0:T(8,128)(2,1)S(1)} %get-tuple-element.166.rest_0_), channel_id=1, source_target_pairs={{0,8},{8,0},{16,24},{24,16},{1,9},{9,1},{17,25},{25,17},{2,10},{10... | collective-permute-start | bytes 2359304 | tf_op jit(solution)/shard_map/ppermute | solution.py:1011
  118.4 21.5 %collective-permute-start.10 = (bf16[4,256,1024]{2,1,0:T(8,128)(2,1)}, bf16[4,256,1024]{2,1,0:T(8,128)(2,1)S(1)}, u32[]{:S(2)}, u32[]{:S(2)}) collective-permute-start(bf16[4,256,1024]{2,1,0:T(8,128)(2,1)} %get-tuple-element.187), channel_id=1, source_target_pairs={{0,1},{1,0},{2,3},{3,2},{4,5},{5,4},{6,7},{7,6},{8,9},{9,8},{10,11... | collective-permute-start | bytes 6291464 | tf_op jit(solution)/shard_map/ppermute | solution.py:1011
  118.5 20.5 %collective-permute-start.11 = (bf16[4,96,1024]{2,1,0:T(8,128)(2,1)}, bf16[4,96,1024]{2,1,0:T(8,128)(2,1)S(1)}, u32[]{:S(2)}, u32[]{:S(2)}) collective-permute-start(bf16[4,96,1024]{2,1,0:T(8,128)(2,1)} %get-tuple-element.188), channel_id=1, source_target_pairs={{0,16},{8,24},{16,0},{24,8},{1,17},{9,25},{17,1},{25,9},{2,18},{10... | collective-permute-start | bytes 2359304 | tf_op jit(solution)/shard_map/ppermute | solution.py:1011
  120.1 19.8 %collective-permute-start.12 = (bf16[4,96,1024]{2,1,0:T(8,128)(2,1)}, bf16[4,96,1024]{2,1,0:T(8,128)(2,1)S(1)}, u32[]{:S(2)}, u32[]{:S(2)}) collective-permute-start(bf16[4,96,1024]{2,1,0:T(8,128)(2,1)} %get-tuple-element.176.rest_0_), channel_id=1, source_target_pairs={{0,8},{8,0},{16,24},{24,16},{1,9},{9,1},{17,25},{25,17},{2,10},{10... | collective-permute-start | bytes 2359304 | tf_op jit(solution)/shard_map/ppermute | solution.py:1011
  154.4 20.3 %collective-permute-start.13 = (bf16[4,384,1024]{2,1,0:T(8,128)(2,1)S(1)}, bf16[4,384,1024]{2,1,0:T(8,128)(2,1)S(1)}, u32[]{:S(2)}, u32[]{:S(2)}) collective-permute-start(bf16[4,384,1024]{2,1,0:T(8,128)(2,1)S(1)} %get-tuple-element.196.rest_0_), channel_id=1, source_target_pairs={{0,1},{1,0},{2,3},{3,2},{4,5},{5,4},{6,7},{7,6},{8,9},{9,8},{10,11... | collective-permute-start | bytes 9437192 | tf_op jit(solution)/shard_map/ppermute | solution.py:1011
  154.5 20.2 %collective-permute-start.14 = (bf16[4,96,1024]{2,1,0:T(8,128)(2,1)}, bf16[4,96,1024]{2,1,0:T(8,128)(2,1)S(1)}, u32[]{:S(2)}, u32[]{:S(2)}) collective-permute-start(bf16[4,96,1024]{2,1,0:T(8,128)(2,1)} %get-tuple-element.197), channel_id=1, source_target_pairs={{0,16},{8,24},{16,0},{24,8},{1,17},{9,25},{17,1},{25,9},{2,18},{10... | collective-permute-start | bytes 2359304 | tf_op jit(solution)/shard_map/ppermute | solution.py:1011
  155.1 19.6 %collective-permute-start.15 = (bf16[4,96,1024]{2,1,0:T(8,128)(2,1)S(1)}, bf16[4,96,1024]{2,1,0:T(8,128)(2,1)S(1)}, u32[]{:S(2)}, u32[]{:S(2)}) collective-permute-start(bf16[4,96,1024]{2,1,0:T(8,128)(2,1)S(1)} %copy-done.67), channel_id=1, source_target_pairs={{0,8},{8,0},{16,24},{24,16},{1,9},{9,1},{17,25},{25,17},{2,10},{10... | collective-permute-start | bytes 2359304 | tf_op jit(solution)/shard_map/ppermute | solution.py:1011
  155.7 15.6 %collective-permute-start.16 = (bf16[2,128,1024]{2,1,0:T(8,128)(2,1)S(1)}, bf16[2,128,1024]{2,1,0:T(8,128)(2,1)S(1)}, u32[]{:S(2)}, u32[]{:S(2)}) collective-permute-start(bf16[2,128,1024]{2,1,0:T(8,128)(2,1)S(1)} %get-tuple-element.199), channel_id=1, source_target_pairs={{0,2},{1,3},{2,0},{3,1},{4,6},{5,7},{6,4},{7,5},{8,10},{9,11},{10,... | collective-permute-start | bytes 1572872 | tf_op jit(solution)/shard_map/ppermute | solution.py:1011
  176.2 24.8 %collective-permute-start.17 = (bf16[4,128,1024]{2,1,0:T(8,128)(2,1)S(1)}, bf16[4,128,1024]{2,1,0:T(8,128)(2,1)S(1)}, u32[]{:S(2)}, u32[]{:S(2)}) collective-permute-start(bf16[4,128,1024]{2,1,0:T(8,128)(2,1)S(1)} %get-tuple-element.206), channel_id=1, source_target_pairs={{0,16},{8,24},{16,0},{24,8},{1,17},{9,25},{17,1},{25,9},{2,18},{10... | collective-permute-start | bytes 3145736 | tf_op jit(solution)/shard_map/ppermute | solution.py:1011
  177.8 24.1 %collective-permute-start.18 = (bf16[4,128,1024]{2,1,0:T(8,128)(2,1)S(1)}, bf16[4,128,1024]{2,1,0:T(8,128)(2,1)S(1)}, u32[]{:S(2)}, u32[]{:S(2)}) collective-permute-start(bf16[4,128,1024]{2,1,0:T(8,128)(2,1)S(1)} %get-tuple-element.201.rest_0_), channel_id=1, source_target_pairs={{0,8},{8,0},{16,24},{24,16},{1,9},{9,1},{17,25},{25,17},{2,10},{10... | collective-permute-start | bytes 3145736 | tf_op jit(solution)/shard_map/ppermute | solution.py:1011
  178.4 15.3 %collective-permute-start.19 = (bf16[1,128,1024]{2,1,0:T(8,128)(2,1)S(1)}, bf16[1,128,1024]{2,1,0:T(8,128)(2,1)S(1)}, u32[]{:S(2)}, u32[]{:S(2)}) collective-permute-start(bf16[1,128,1024]{2,1,0:T(8,128)(2,1)S(1)} %get-tuple-element.207), channel_id=1, source_target_pairs={{0,4},{1,5},{2,6},{3,7},{4,0},{5,1},{6,2},{7,3},{8,12},{9,13},{10,... | collective-permute-start | bytes 786440 | tf_op jit(solution)/shard_map/ppermute | solution.py:1011
  205.1 21.9 %collective-permute-start.20 = (bf16[4,128,1024]{2,1,0:T(8,128)(2,1)S(1)}, bf16[4,128,1024]{2,1,0:T(8,128)(2,1)S(1)}, u32[]{:S(2)}, u32[]{:S(2)}) collective-permute-start(bf16[4,128,1024]{2,1,0:T(8,128)(2,1)S(1)} %get-tuple-element.211.refs_12_), channel_id=1, source_target_pairs={{0,1},{1,0},{2,3},{3,2},{4,5},{5,4},{6,7},{7,6},{8,9},{9,8},{10,11... | collective-permute-start | bytes 3145736 | tf_op jit(solution)/shard_map/ppermute | solution.py:1011
  205.2 21.8 %collective-permute-start.21 = (bf16[2,128,1024]{2,1,0:T(8,128)(2,1)S(1)}, bf16[2,128,1024]{2,1,0:T(8,128)(2,1)S(1)}, u32[]{:S(2)}, u32[]{:S(2)}) collective-permute-start(bf16[2,128,1024]{2,1,0:T(8,128)(2,1)S(1)} %get-tuple-element.213), channel_id=1, source_target_pairs={{0,2},{1,3},{2,0},{3,1},{4,6},{5,7},{6,4},{7,5},{8,10},{9,11},{10,... | collective-permute-start | bytes 1572872 | tf_op jit(solution)/shard_map/ppermute | solution.py:1011
  208.2 18.0 %collective-permute-start.22 = (bf16[4,48,1024]{2,1,0:T(8,128)(2,1)S(1)}, bf16[4,48,1024]{2,1,0:T(8,128)(2,1)S(1)}, u32[]{:S(2)}, u32[]{:S(2)}) collective-permute-start(bf16[4,48,1024]{2,1,0:T(8,128)(2,1)S(1)} %get-tuple-element.209.refs_4_), channel_id=1, source_target_pairs={{0,8},{8,0},{16,24},{24,16},{1,9},{9,1},{17,25},{25,17},{2,10},{10... | collective-permute-start | bytes 1179656 | tf_op jit(solution)/shard_map/ppermute | solution.py:1011
  209.4 17.6 %collective-permute-start.23 = (bf16[4,48,1024]{2,1,0:T(8,128)(2,1)S(1)}, bf16[4,48,1024]{2,1,0:T(8,128)(2,1)S(1)}, u32[]{:S(2)}, u32[]{:S(2)}) collective-permute-start(bf16[4,48,1024]{2,1,0:T(8,128)(2,1)S(1)} %get-tuple-element.215), channel_id=1, source_target_pairs={{0,16},{8,24},{16,0},{24,8},{1,17},{9,25},{17,1},{25,9},{2,18},{10... | collective-permute-start | bytes 1179656 | tf_op jit(solution)/shard_map/ppermute | solution.py:1011
  225.0 21.4 %collective-permute-start.28 = (bf16[1,128,1024]{2,1,0:T(8,128)(2,1)S(1)}, bf16[1,128,1024]{2,1,0:T(8,128)(2,1)S(1)}, u32[]{:S(2)}, u32[]{:S(2)}) collective-permute-start(bf16[1,128,1024]{2,1,0:T(8,128)(2,1)S(1)} %get-tuple-element.226.refs_0_), channel_id=1, source_target_pairs={{0,16},{8,24},{16,0},{24,8},{1,17},{9,25},{17,1},{25,9},{2,18},{10... | collective-permute-start | bytes 786440 | tf_op jit(solution)/shard_map/ppermute | solution.py:1011
  226.2 20.2 %collective-permute-start.29 = (bf16[1,128,1024]{2,1,0:T(8,128)(2,1)S(1)}, bf16[1,128,1024]{2,1,0:T(8,128)(2,1)S(1)}, u32[]{:S(2)}, u32[]{:S(2)}) collective-permute-start(bf16[1,128,1024]{2,1,0:T(8,128)(2,1)S(1)} %collective-permute-done.27.refs_29_.refs_1_), channel_id=1, source_target_pairs={{0,16},{8,24},{16,0},{24,8},{1,17},{9,25},{17,1},{25,9},{2,18},{10... | collective-permute-start | bytes 786440 | tf_op jit(solution)/shard_map/ppermute | solution.py:1011
  228.0 18.4 %collective-permute-start.24 = (bf16[4,32,1024]{2,1,0:T(8,128)(2,1)S(1)}, bf16[4,32,1024]{2,1,0:T(8,128)(2,1)S(1)}, u32[]{:S(2)}, u32[]{:S(2)}) collective-permute-start(bf16[4,32,1024]{2,1,0:T(8,128)(2,1)S(1)} %get-tuple-element.224), channel_id=1, source_target_pairs={{0,16},{8,24},{16,0},{24,8},{1,17},{9,25},{17,1},{25,9},{2,18},{10... | collective-permute-start | bytes 786440 | tf_op jit(solution)/shard_map/ppermute | solution.py:1011
  229.3 17.1 %collective-permute-start.25 = (bf16[4,32,1024]{2,1,0:T(8,128)(2,1)S(1)}, bf16[4,32,1024]{2,1,0:T(8,128)(2,1)S(1)}, u32[]{:S(2)}, u32[]{:S(2)}) collective-permute-start(bf16[4,32,1024]{2,1,0:T(8,128)(2,1)S(1)} %get-tuple-element.216.refs_12_), channel_id=1, source_target_pairs={{0,8},{8,0},{16,24},{24,16},{1,9},{9,1},{17,25},{25,17},{2,10},{10... | collective-permute-start | bytes 786440 | tf_op jit(solution)/shard_map/ppermute | solution.py:1011
  230.1 16.3 %collective-permute-start.26 = (bf16[1,128,1024]{2,1,0:T(8,128)(2,1)S(1)}, bf16[1,128,1024]{2,1,0:T(8,128)(2,1)S(1)}, u32[]{:S(2)}, u32[]{:S(2)}) collective-permute-start(bf16[1,128,1024]{2,1,0:T(8,128)(2,1)S(1)} %get-tuple-element.225), channel_id=1, source_target_pairs={{0,4},{1,5},{2,6},{3,7},{4,0},{5,1},{6,2},{7,3},{8,12},{9,13},{10,... | collective-permute-start | bytes 786440 | tf_op jit(solution)/shard_map/ppermute | solution.py:1011
  286.6 19.2 %collective-permute-start.47 = (bf16[1,128,1024]{2,1,0:T(8,128)(2,1)S(1)}, bf16[1,128,1024]{2,1,0:T(8,128)(2,1)S(1)}, u32[]{:S(2)}, u32[]{:S(2)}) collective-permute-start(bf16[1,128,1024]{2,1,0:T(8,128)(2,1)S(1)} %get-tuple-element.245.refs_0_), channel_id=1, source_target_pairs={{0,16},{8,24},{16,0},{24,8},{1,17},{9,25},{17,1},{25,9},{2,18},{10... | collective-permute-start | bytes 786440 | tf_op jit(solution)/shard_map/ppermute | solution.py:1011
  (115 other events, 1120.3 us)
where the time goes:
time: 348 us; the launch traced here: 341 us
  Pallas kernels  170 us (49%)
  waiting for transfers between devices  88.1 us (25%)
  starting transfers between devices  59.1 us (17%)
  local copies, waits for them, and re-layouts  19.5 us (6%)
    ppermute x56, waiting for transfers between devices, permute(): return lax.ppermute(value, axis, [(i, to(i)) for i in range(size)])  88.1 us
    ppermute x56, starting transfers between devices, permute(): return lax.ppermute(value, axis, [(i, to(i)) for i in range(size)])  59.1 us
    pallas_call x4, Pallas kernels, mlp_packed(): pl.pallas_call(mlp_packed_kernel, grid_spec=pltpu.PrefetchScalarGridSpec(...  42.6 us
    pallas_call x2, Pallas kernels, token_backward(): pl.pallas_call(functools.partial(each_head, token_backward_kernel, heads,...  24.1 us
    pallas_call x15, Pallas kernels, blend(): pl.pallas_call(kernel, grid_spec=pltpu.PrefetchScalarGridSpec(num_scalar_...  20.5 us
    unnamed x166, local copies, waits for them, and re-layouts  17.9 us
    pallas_call x1, Pallas kernels, attention_forward(): pl.pallas_call(functools.partial(each_head, attention_forward_kernel, hea...  15.4 us
    pallas_call x2, Pallas kernels, single(): pl.pallas_call(kernel, grid=(1,), in_specs=[one_block(a) for a in ins] +...  13.7 us
  transfers between devices with their start and end apart: 56, of which 25 were waited for; matrix products, arithmetic and copies ran while one was open for 0% of the time, Pallas kernels for 27%

commit v1 on v0

--- a/solution.py
+++ b/solution.py
@@ -39,7 +39,7 @@
     return lax.dot_general(a, b, dims, preferred_element_type=f32)
 
 
-def params(mib=26):
+def params(mib=18):
     return pltpu.CompilerParams(
         dimension_semantics=("arbitrary",), vmem_limit_bytes=mib * 1024 * 1024
     )
@@ -810,10 +810,10 @@
     return unit, jnp.broadcast_to(inv, (value.shape[0], 128))
 
 
-def table_kernel(table, gain, weight, unit_out, inv_out, normed_out, qkv_out):
-    step = pl.program_id(0)
-
-    @pl.when(step == 0)
+def table_kernel(table, gain, weight, *rest):
+    unit_out, inv_out, normed_out, qkv_out = rest[-4:]
+
+    @pl.when(pl.program_id(0) == 0)
     def _():
         unit, inv = unit_of(table[...].astype(f32))
         unit_out[...] = unit
@@ -823,11 +823,15 @@
     qkv_out[...] = dot(normed_out[...], weight[...]).astype(bf16)
 
 
+def table_more_kernel(normed, weight, *rest):
+    rest[-1][...] = dot(normed[...], weight[...]).astype(bf16)
+
+
 def table_forward(table, gain, weight):
     flat = lambda *shape: pl.BlockSpec(shape, lambda g: (0, 0))
     return pl.pallas_call(
         table_kernel,
-        grid=(6,),
+        grid=(2,),
         in_specs=[
             flat(VOCAB, D),
             flat(1, D),
@@ -842,13 +846,31 @@
         out_shape=[
             kept(f32, VOCAB, D),
             kept(f32, VOCAB, 128),
-            kept(bf16, VOCAB, D),
+            like(bf16, VOCAB, D),
             like(bf16, VOCAB, 3 * D),
         ],
         compiler_params=params(),
         cost_estimate=cost(1e3, 1e3),
         name="table_forward",
     )(*stays(table), gain, *stays(weight))
+
+
+def table_more(third, normed, weight, onto, deps=()):
+    return pl.pallas_call(
+        table_more_kernel,
+        grid=(2,),
+        in_specs=[
+            pl.BlockSpec((VOCAB, D), lambda g: (0, 0)),
+            pl.BlockSpec((D, D // 2), lambda g: (0, 2 * third + g)),
+        ]
+        + [pl.BlockSpec(memory_space=pl.ANY)] * (1 + len(deps)),
+        out_specs=pl.BlockSpec((VOCAB, D // 2), lambda g: (0, 2 * third + g)),
+        out_shape=like(bf16, VOCAB, 3 * D),
+        input_output_aliases={2: 0},
+        compiler_params=params(),
+        cost_estimate=cost(1e3, 1e3),
+        name="table_more",
+    )(normed, *stays(weight), onto, *deps)
 
 
 def states_forward_kernel(states, gain, weight, unit_out, inv_out, normed_out, kv_out):
@@ -1156,6 +1178,15 @@
         ] + [(array, self.rows, lambda g, s: (0, 0)) for array in extra]
         return [((1, self.rows, self.columns), self.rows, 1, [sources])]
 
+    def doubled(self, step):
+        if step == 1:
+            sources = [w.quarters(lambda g, s: g) for w in self.parts]
+        else:
+            sources = [
+                [(a, self.rows, lambda g, s: (g, 0)) for a in (self.sum, self.other)]
+            ]
+        return [((4, self.rows, self.columns), self.rows, 4, sources)]
+
     def far(self):
         return self.rest(lambda s: 1 - s[ZI] // 2)
 
@@ -1173,7 +1204,7 @@
         self.pending.append(came)
         return came
 
-    def boundary(self, after, first=(), second=(), near=(), far=(), close=(), swap=(), join=()):
+    def boundary(self, after, first=(), second=(), near=(), far=(), close=(), swap=(), join=(), double=None):
         outs, sent = [], []
         for axis in (XI, YI):
             groups = {}
@@ -1193,6 +1224,8 @@
         for columns, step in ((near, Column.near), (far, Column.far), (close, Column.close)):
             for c in columns:
                 outs += step(c)
+        if double:
+            outs += double[0].doubled(double[1])
         if join:
             segments = [c.close()[0][3][0] for c in join]
             total = sum(c.rows for c in join)
@@ -1218,6 +1251,12 @@
             self.pending.append(c.from_far)
         for c in close:
             c.own = results.pop(0)
+        if double:
+            column, step = double
+            column.sum = results.pop(0)
+            if step < 3:
+                column.other = permute(column.sum, "seq", lambda i: i ^ (2 * step))
+                self.pending.append(column.other)
         if join:
             self.joined = results.pop(0)
         self.swapped = [self.swap(send) for send in results]
@@ -1383,29 +1422,6 @@
         cost_estimate=cost(1e3, 1e3),
         name="unpack_mlp",
     )(places, *flat)
-
-
-def ring_rows(places, parts, deps=()):
-    def kernel(s, *refs):
-        out = refs[-1]
-        for k in range(4):
-            out[pl.ds(s[ZI] ^ k, 1)] = refs[k][...]
-
-    shape = (4,) + parts[0].shape[1:]
-    return pl.pallas_call(
-        kernel,
-        grid_spec=pltpu.PrefetchScalarGridSpec(
-            num_scalar_prefetch=1,
-            grid=(1,),
-            in_specs=[whole(p) for p in parts]
-            + [pl.BlockSpec(memory_space=pl.ANY)] * len(deps),
-            out_specs=pl.BlockSpec(shape, lambda g, s: (0, 0, 0)),
-        ),
-        out_shape=jax.ShapeDtypeStruct(shape, bf16),
-        compiler_params=params(),
-        cost_estimate=cost(1e3, 1e3),
-        name="ring_rows",
-    )(places, *parts, *deps)
 
 
 def stack_rows(places, parts, deps=()):
@@ -1564,7 +1580,16 @@
         bias_out[h] = table[h : h + 1]
 
 
-def prepare(places, char_ids, seg_starts, gate_logit, distance_bias, deps=()):
+def side_by_side(mine, other, deps):
+    def kernel(a, b, *rest):
+        rest[-1][: a.shape[0]] = a[...]
+        rest[-1][a.shape[0] :] = b[...]
+
+    out = like(mine.dtype, 2 * mine.shape[0], *mine.shape[1:])
+    return single(kernel, "side_by_side", (mine, other), (out,), deps=deps)[0]
+
+
+def prepare(places, char_ids, seg_starts, gate_logit, distance_bias, table_parts):
     packed = jnp.concatenate(
         [
             char_ids.reshape(4, 128),
@@ -1573,11 +1598,13 @@
         ],
         axis=0,
     )[None]
-    for bit in (1, 2):
-        packed = jnp.concatenate(
-            [packed, permute(packed, "seq", lambda i, bit=bit: i ^ bit)], axis=0
-        )
+    done = ()
+    for bit, part in zip((1, 2), table_parts):
+        came = permute(packed, "seq", lambda i, bit=bit: i ^ bit)
+        done = part(done)
+        packed = side_by_side(packed, came, done)
     beyond = permute(packed, "seq", lambda i: i ^ 4)
+    deps = table_parts[2](done)
     ins = (
         packed,
         beyond,
@@ -1596,7 +1623,7 @@
         like(f32, 1, D),
         like(f32, HEADS, 1, CONTEXT),
     )
-    return pl.pallas_call(
+    prepared = pl.pallas_call(
         prepare_kernel,
         grid_spec=pltpu.PrefetchScalarGridSpec(
             num_scalar_prefetch=1,
@@ -1611,6 +1638,7 @@
         cost_estimate=cost(1e3, 1e3),
         name="prepare",
     )(places, *ins, *deps)
+    return (*prepared, deps[0])
 
 
 def plain_prepare(char_ids, seg_starts, gate_logit, distance_bias):
@@ -1675,13 +1703,19 @@
     table_unit, table_inv, normed_table, qkv_table = table_forward(
         char_table, norm_gain, qkv_weight
     )
+    more = lambda third: lambda done: (
+        table_more(third, normed_table, qkv_weight, done[0]),
+    )
+    table_parts = (lambda done: (qkv_table,), more(1), more(2))
 
     characters = (char_ids, seg_starts, gate_logit, distance_bias)
     if fitted():
         places = places_of()
-        prepared = prepare(places, *characters, (qkv_table,))
+        *prepared, qkv_table = prepare(places, *characters, table_parts)
     else:
         prepared = plain_prepare(*characters)
+        for part in table_parts:
+            (qkv_table,) = part((qkv_table,))
     span, live, counts, count_rows, pick, pick_t, forget, bias_rows = prepared
     states_in, forget_slope, lowest = summary_forward(
         span, state_query, qkv_table, counts, count_rows, state_init, forget
@@ -1748,43 +1782,35 @@
     onto = summary_backward(*summary_args, (send,), 0)
     mark = traffic.boundary((onto[0],), middle, parts[3], far=[front])
     g, gsq, ginit = summary_backward(*summary_args, (mark,), 1, onto)
-    mark = traffic.boundary((g,), (), middle, near=[back], close=[front])
     send, keep = packed_pair(
-        "pack_states", places, [gsq.reshape(8, 64, D), ginit.reshape(8, 64, D)], (mark,)
-    )
-    states = wings(keep, traffic.swap(send))
+        "pack_states", places, [gsq.reshape(8, 64, D), ginit.reshape(8, 64, D)]
+    )
+    mark = traffic.boundary((), (), middle, near=[back], close=[front], swap=[send])
+    states = wings(keep, traffic.swapped[0])
     tokens_args = (
         v.live, v.pick, v.pick_t, v.qkv_table, v.bias_rows, v.lse, inner, grad_mixed, gq
     )
-    onto = token_backward(*tokens_args, (send,), 0)
+    onto = token_backward(*tokens_args, (mark,), 0)
     mark = traffic.boundary((onto[1],), states, far=[back])
     front_rows = traffic.spread(front.own)
     g_tokens, fold = token_backward(*tokens_args, (mark,), 1, onto)
     side, rest = Column(middle), Column(states)
-    mark = traffic.boundary((fold,), (), states, near=[side], close=[back])
     send, keep = pack_rows(
-        places, mark, g_tokens, g, rows_sum, grad_mlp_gain, grad_state_gain, grad_gate, fold
-    )
-    rows = wings(keep, traffic.swap(send))
+        places, fold, g_tokens, g, rows_sum, grad_mlp_gain, grad_state_gain, grad_gate, fold
+    )
+    traffic.boundary((), (), states, near=[side], close=[back], swap=[send])
+    rows = wings(keep, traffic.swapped[0])
     last = Column(rows)
     traffic.boundary((), rows, near=[rest], far=[side])
     traffic.boundary((), (), rows, far=[rest])
     back_rows = traffic.spread(back.own, 2)
-    traffic.boundary((), near=[last], join=[side, rest])
+    traffic.boundary((), double=(last, 1), join=[side, rest])
     side_own = traffic.joined
-    traffic.boundary((), far=[last])
+    traffic.boundary((), double=(last, 2))
     side_rows = traffic.spread(side_own)
     grad_down, grad_up, mark = unpack_mlp(places, [front_rows, back_rows])
-    traffic.boundary((mark,), close=[last])
-    beside = permute(last.own, "seq", lambda i: i ^ 2)
-    row_ring = [
-        last.own,
-        beside,
-        permute(last.own, "seq", lambda i: i ^ 4),
-        permute(beside, "seq", lambda i: i ^ 4),
-    ]
-    ring = ring_rows(places, row_ring)
-    ring_parts = traffic.spread(ring)
+    traffic.boundary((mark,), double=(last, 3))
+    ring_parts = traffic.spread(last.sum)
     grad_state_kv, grad_out, grad_state_query, grad_state_init, mark = unpack(
         "unpack_side",
         places,

time: 348 us -> 335 us (0.963)
  local copies, waits for them, and re-layouts: 19.5 us -> 11.8 us
  Pallas kernels: 170 us -> 166 us
    unnamed x166 -> x126, local copies, waits for them, and re-layouts: 17.9 us -> 10.3 us
    ppermute x56 -> x53, starting transfers between devices: 59.1 us -> 61.9 us  [permute(): return lax.ppermute(value, axis, [(i, to(i)) for i in range(size)])]
    ppermute x56 -> x53, waiting for transfers between devices: 88.1 us -> 85.6 us  [permute(): return lax.ppermute(value, axis, [(i, to(i)) for i in range(size)])]
    pallas_call x2 -> x4, Pallas kernels: 13.7 us -> 13.4 us  [single(): pl.pallas_call(kernel, grid=(1,), in_specs=[one_block(a) for a in ins] +...]
    pallas_call x2 -> x3, Pallas kernels: 7.58 us -> 7.59 us  [the longest x2 4.36 us: table_more(): pl.pallas_call(table_more_kernel, grid=(2,), in_specs=[pl.BlockSpec((VOCA...]
  transfers between devices with their start and end apart: 56 -> 53, of which waited for: 25 -> 25; matrix products, arithmetic and copies ran while one was open for 0% -> 0% of each run, Pallas kernels for 27% -> 29%
where the time goes in v1:
time: 335 us; the launch traced here: 329 us
  Pallas kernels  166 us (50%)
  waiting for transfers between devices  85.6 us (26%)
  starting transfers between devices  61.9 us (18%)
  local copies, waits for them, and re-layouts  11.8 us (4%)
    ppermute x53, waiting for transfers between devices, permute(): return lax.ppermute(value, axis, [(i, to(i)) for i in range(size)])  85.6 us
    ppermute x53, starting transfers between devices, permute(): return lax.ppermute(value, axis, [(i, to(i)) for i in range(size)])  61.9 us
    pallas_call x4, Pallas kernels, mlp_packed(): pl.pallas_call(mlp_packed_kernel, grid_spec=pltpu.PrefetchScalarGridSpec(...  41.1 us
    pallas_call x2, Pallas kernels, token_backward(): pl.pallas_call(functools.partial(each_head, token_backward_kernel, heads,...  24.2 us
    pallas_call x15, Pallas kernels, blend(): pl.pallas_call(kernel, grid_spec=pltpu.PrefetchScalarGridSpec(num_scalar_...  17.9 us
    pallas_call x1, Pallas kernels, attention_forward(): pl.pallas_call(functools.partial(each_head, attention_forward_kernel, hea...  15.4 us
    pallas_call x4, Pallas kernels, single(): pl.pallas_call(kernel, grid=(1,), in_specs=[one_block(a) for a in ins] +...  13.4 us
    pallas_call x1, Pallas kernels, state_backward(): pl.pallas_call(functools.partial(each_head, state_backward_kernel, heads,...  10.8 us
  transfers between devices with their start and end apart: 53, of which 25 were waited for; matrix products, arithmetic and copies ran while one was open for 0% of the time, Pallas kernels for 29%

profile of v1, /device:TPU:0, one launch (start us, length us, event | category | flops | bytes accessed | tf_op | source)
XLA Modules:
  0.0 329.5 jit_solution(11635567473557335818)
XLA Ops:
  18.6 6.2 %summary_forward.1 = (f32[512,1024]{1,0:T(8,128)S(1)}, f32[512,1024]{1,0:T(8,128)}, f32[2,8,128]{2,1,0:T(8,128)S(1)}) custom-call(s32[2]{0:T(128)S(1)} %get-tuple-element.143.span, bf16[512,1024]{1,0:T(8,128)(2,1)S(1)} %copy-done.18, bf16[256,3072]{1,0:T(8,128)(2,1)S(1)} %table_more.3.rest_0_.kt.vt.refs_3_.refs_4_.refs_5_.refs_1_, ...), custom_call_target="tpu_custom_call" | custom-call | flops 1000 | bytes 1000 | tf_op jit(solution)/shard_map/summary_forward/pallas_call | solution.py:195
  24.8 4.9 %states_forward.1 = (f32[512,1024]{1,0:T(8,128)}, f32[512,128]{1,0:T(8,128)}, bf16[512,1024]{1,0:T(8,128)(2,1)}, bf16[512,2048]{1,0:T(8,128)(2,1)S(1)}) custom-call(f32[512,1024]{1,0:T(8,128)S(1)} %get-tuple-element.147.states, f32[1,1024]{1,0:T(1,128)S(1)} %bitcast.53, bf16[1024,2048]{1,0:T(8,128)(2,1)S(1)} %copy-done.13), custom_call_target="tpu_custom_call" | custom-call | flops 1000 | bytes 1000 | tf_op jit(solution)/shard_map/states_forward/pallas_call | solution.py:891
  29.8 15.4 %attention_forward.1 = (bf16[512,1024]{1,0:T(8,128)(2,1)S(1)}, f32[8,1,512]{2,1,0:T(1,128)S(1)}) custom-call(s32[1]{0:T(128)} %get-tuple-element.140.refs_0_, bf16[1024,256]{1,0:T(8,128)(2,1)S(1)} %get-tuple-element.141.refs_1_.pick.refs_0_, bf16[256,1024]{1,0:T(8,128)(2,1)S(1)} %get-tuple-element.142.refs_2_, ...), custom_call_target="tpu_custom_call" | custom-call | flops 1000 | bytes 1000 | tf_op jit(solution)/shard_map/attention_forward/pallas_call | solution.py:410
  45.3 4.1 %residual_forward.1 = (f32[512,1024]{1,0:T(8,128)S(1)}, f32[512,1024]{1,0:T(8,128)}, f32[512,128]{1,0:T(8,128)}, bf16[512,1024]{1,0:T(8,128)(2,1)S(1)}, bf16[2,512,512]{2,1,0:T(8,128)(2,1)S(1)}) custom-call(s32[6]{0:T(128)S(1)} %stack.27.places.s, bf16[512,1024]{1,0:T(8,128)(2,1)S(1)} %get-tuple-element.150.mixed.refs_5_, bf16[1024,1024]{1,0:T(8,128)(2,1)S(1)} %copy-done.28, ...), custom_call_target="tpu_custom_call" | custom-call | flops 1000 | bytes 1000 | tf_op jit(solution)/shard_map/residual_forward/pallas_call | solution.py:943
  51.0 10.0 %feed_forward.4 = (bf16[4,256,1024]{2,1,0:T(8,128)(2,1)S(1)}, bf16[4,256,1024]{2,1,0:T(8,128)(2,1)S(1)}, f32[512,1024]{1,0:T(8,128)S(1)}, f32[512,1024]{1,0:T(8,128)S(1)}) custom-call(s32[6]{0:T(128)S(1)} %stack.27.places.s, bf16[512,1024]{1,0:T(8,128)(2,1)S(1)} %get-tuple-element.151.x, bf16[2,512,512]{2,1,0:T(8,128)(2,1)S(1)} %get-tuple-element.152.xs, ...), custom_call_target="tpu_custom_call" | custom-call | flops 1000 | bytes 1000 | tf_op jit(solution)/shard_map/feed_forward/pallas_call | solution.py:746
  61.1 10.2 %feed_forward.5 = (bf16[4,256,1024]{2,1,0:T(8,128)(2,1)S(1)}, bf16[4,256,1024]{2,1,0:T(8,128)(2,1)S(1)}, f32[512,1024]{1,0:T(8,128)S(1)}, f32[512,1024]{1,0:T(8,128)S(1)}) custom-call(s32[6]{0:T(128)S(1)} %stack.27.places.s, bf16[512,1024]{1,0:T(8,128)(2,1)S(1)} %get-tuple-element.151.x, bf16[2,512,512]{2,1,0:T(8,128)(2,1)S(1)} %get-tuple-element.152.xs, ...), custom_call_target="tpu_custom_call" | custom-call | flops 1000 | bytes 1000 | tf_op jit(solution)/shard_map/feed_forward/pallas_call | solution.py:746
  76.3 11.0 %feed_forward.6 = (bf16[4,256,1024]{2,1,0:T(8,128)(2,1)}, bf16[4,256,1024]{2,1,0:T(8,128)(2,1)S(1)}, f32[512,1024]{1,0:T(8,128)S(1)}, f32[512,1024]{1,0:T(8,128)S(1)}) custom-call(s32[6]{0:T(128)S(1)} %stack.27.places.s, bf16[512,1024]{1,0:T(8,128)(2,1)S(1)} %get-tuple-element.151.x, bf16[2,512,512]{2,1,0:T(8,128)(2,1)S(1)} %get-tuple-element.152.xs, ...), custom_call_target="tpu_custom_call" | custom-call | flops 1000 | bytes 1000 | tf_op jit(solution)/shard_map/feed_forward/pallas_call | solution.py:746
  93.7 10.0 %feed_forward.7 = (bf16[4,256,1024]{2,1,0:T(8,128)(2,1)S(1)}, bf16[4,256,1024]{2,1,0:T(8,128)(2,1)S(1)}, f32[512,1024]{1,0:T(8,128)S(1)}, f32[512,1024]{1,0:T(8,128)S(1)}) custom-call(s32[6]{0:T(128)S(1)} %stack.27.places.s, bf16[512,1024]{1,0:T(8,128)(2,1)S(1)} %get-tuple-element.151.x, bf16[2,512,512]{2,1,0:T(8,128)(2,1)S(1)} %copy-done.12, ...), custom_call_target="tpu_custom_call" | custom-call | flops 1000 | bytes 1000 | tf_op jit(solution)/shard_map/feed_forward/pallas_call | solution.py:746
  122.3 10.8 %state_backward.1 = (bf16[512,1024]{1,0:T(8,128)(2,1)}, bf16[512,1024]{1,0:T(8,128)(2,1)}, f32[8,128,512]{2,1,0:T(8,128)S(1)}, f32[8,1,512]{2,1,0:T(1,128)S(1)}) custom-call(bf16[1024,256]{1,0:T(8,128)(2,1)S(1)} %copy-done.10, bf16[256,3072]{1,0:T(8,128)(2,1)S(1)} %table_more.3.rest_0_.kt.vt.refs_3_.refs_4_.refs_5_.refs_1_, bf16[512,2048]{1,0:T(8,128)(2,1)S(1)} %copy-done.5, ...), custom_call_target="tpu_custom_call" | custom-call | flops 1000 | bytes 1000 | tf_op jit(solution)/shard_map/state_backward/pallas_call | solution.py:484
  136.7 9.7 %states_back.1 = (bf16[1024,1024]{1,0:T(8,128)(2,1)S(1)}, bf16[1024,1024]{1,0:T(8,128)(2,1)S(1)}, f32[1,1024]{1,0:T(1,128)S(1)}, f32[512,1024]{1,0:T(8,128)S(1)}, f32[1,1024]{1,0:T(1,128)S(1)}) custom-call(bf16[512,1024]{1,0:T(8,128)(2,1)} %get-tuple-element.182.gsk, bf16[512,1024]{1,0:T(8,128)(2,1)} %get-tuple-element.183.gsv, bf16[1024,2048]{1,0:T(8,128)(2,1)} %weight.10, ...), custom_call_target="tpu_custom_call" | custom-call | flops 1000 | bytes 1000 | tf_op jit(solution)/shard_map/states_back/pallas_call | solution.py:782
  155.5 8.8 %collective-permute-done.16.refs_11_.refs_15_.refs_39_ = bf16[2,128,1024]{2,1,0:T(8,128)(2,1)S(1)} collective-permute-done((bf16[2,128,1024]{2,1,0:T(8,128)(2,1)S(1)}, bf16[2,128,1024]{2,1,0:T(8,128)(2,1)S(1)}, u32[]{:S(2)}, u32[]{:S(2)}) %collective-permute-start.16) | collective-permute-done | bytes 524320 | tf_op jit(solution)/shard_map/ppermute | solution.py:1033
  172.3 5.6 %collective-permute-start.19 = (bf16[1,128,1024]{2,1,0:T(8,128)(2,1)S(1)}, bf16[1,128,1024]{2,1,0:T(8,128)(2,1)S(1)}, u32[]{:S(2)}, u32[]{:S(2)}) collective-permute-start(bf16[1,128,1024]{2,1,0:T(8,128)(2,1)S(1)} %get-tuple-element.210), channel_id=1, source_target_pairs={{0,4},{1,5},{2,6},{3,7},{4,0},{5,1},{6,2},{7,3},{8,12},{9,13},{10,... | collective-permute-start | bytes 786440 | tf_op jit(solution)/shard_map/ppermute | solution.py:1033
  182.3 6.5 %collective-permute-done.19.refs_40_.refs_43_ = bf16[1,128,1024]{2,1,0:T(8,128)(2,1)S(1)} collective-permute-done((bf16[1,128,1024]{2,1,0:T(8,128)(2,1)S(1)}, bf16[1,128,1024]{2,1,0:T(8,128)(2,1)S(1)}, u32[]{:S(2)}, u32[]{:S(2)}) %collective-permute-start.19) | collective-permute-done | bytes 262176 | tf_op jit(solution)/shard_map/ppermute | solution.py:1033
  188.8 5.1 %collective-permute-done.17.refs_2_.refs_17_.refs_33_.refs_42_.refs_12_.refs_20_ = bf16[4,128,1024]{2,1,0:T(8,128)(2,1)S(1)} collective-permute-done((bf16[4,128,1024]{2,1,0:T(8,128)(2,1)S(1)}, bf16[4,128,1024]{2,1,0:T(8,128)(2,1)S(1)}, u32[]{:S(2)}, u32[]{:S(2)}) %collective-permute-start.17) | collective-permute-done | bytes 1048608 | tf_op jit(solution)/shard_map/ppermute | solution.py:1033
  202.3 12.0 %token_backward.2 = (f32[8,256,384]{2,1,0:T(8,128)S(1)}, f32[8,1,128]{2,1,0:T(1,128)S(1)}) custom-call(s32[1]{0:T(128)} %get-tuple-element.140.refs_0_, bf16[1024,256]{1,0:T(8,128)(2,1)S(1)} %copy-done.10, bf16[256,1024]{1,0:T(8,128)(2,1)S(1)} %copy-done.38, bf16[256,3072]{1,0:T(8,128)(2,1)S(1)} %table_more.3.rest_0_.kt.vt.refs_3_.refs_4_.refs_5_.refs_1_, ...), custom_call_target="tpu_custom_call" | custom-call | flops 1000 | bytes 1000 | tf_op jit(solution)/shard_map/token_backward/pallas_call | solution.py:594
  221.7 6.5 %collective-permute-start.26 = (bf16[1,128,1024]{2,1,0:T(8,128)(2,1)S(1)}, bf16[1,128,1024]{2,1,0:T(8,128)(2,1)S(1)}, u32[]{:S(2)}, u32[]{:S(2)}) collective-permute-start(bf16[1,128,1024]{2,1,0:T(8,128)(2,1)S(1)} %get-tuple-element.229), channel_id=1, source_target_pairs={{0,4},{1,5},{2,6},{3,7},{4,0},{5,1},{6,2},{7,3},{8,12},{9,13},{10,... | collective-permute-start | bytes 786440 | tf_op jit(solution)/shard_map/ppermute | solution.py:1033
  228.2 12.2 %token_backward.3 = (f32[8,256,384]{2,1,0:T(8,128)S(1)}, f32[8,1,128]{2,1,0:T(1,128)S(1)}) custom-call(s32[1]{0:T(128)} %get-tuple-element.140.refs_0_, bf16[1024,256]{1,0:T(8,128)(2,1)S(1)} %copy-done.10, bf16[256,1024]{1,0:T(8,128)(2,1)S(1)} %copy-done.38, ...), custom_call_target="tpu_custom_call", output_to_operand_aliasing={{0}: (13, {}), {1}: (14, {})} | custom-call | flops 1000 | bytes 1000 | tf_op jit(solution)/shard_map/token_backward/pallas_call | solution.py:594
  250.3 4.5 %collective-permute-done.33.refs_21_.refs_24_.refs_9_ = bf16[2,96,1024]{2,1,0:T(8,128)(2,1)S(1)} collective-permute-done((bf16[2,96,1024]{2,1,0:T(8,128)(2,1)S(1)}, bf16[2,96,1024]{2,1,0:T(8,128)(2,1)S(1)}, u32[]{:S(2)}, u32[]{:S(2)}) %collective-permute-start.33) | collective-permute-done | bytes 393248 | tf_op jit(solution)/shard_map/ppermute | solution.py:1033
  259.7 4.7 %collective-permute-done.36.refs_7_.refs_10_.refs_12_ = bf16[2,32,1024]{2,1,0:T(8,128)(2,1)S(1)} collective-permute-done((bf16[2,32,1024]{2,1,0:T(8,128)(2,1)S(1)}, bf16[2,32,1024]{2,1,0:T(8,128)(2,1)S(1)}, u32[]{:S(2)}, u32[]{:S(2)}) %collective-permute-start.36) | collective-permute-done | bytes 131104 | tf_op jit(solution)/shard_map/ppermute | solution.py:1033
  272.2 4.9 %collective-permute-done.43.refs_19_.refs_7_ = bf16[1,128,1024]{2,1,0:T(8,128)(2,1)S(1)} collective-permute-done((bf16[1,128,1024]{2,1,0:T(8,128)(2,1)S(1)}, bf16[1,128,1024]{2,1,0:T(8,128)(2,1)S(1)}, u32[]{:S(2)}, u32[]{:S(2)}) %collective-permute-start.43) | collective-permute-done | bytes 262176 | tf_op jit(solution)/shard_map/ppermute | solution.py:1033
  280.7 6.9 %collective-permute-done.44.refs_1_.refs_2_ = bf16[4,96,384]{2,1,0:T(8,128)(2,1)S(1)} collective-permute-done((bf16[4,96,384]{2,1,0:T(8,128)(2,1)S(1)}, bf16[4,96,384]{2,1,0:T(8,128)(2,1)S(1)}, u32[]{:S(2)}, u32[]{:S(2)}) %collective-permute-start.44) | collective-permute-done | bytes 294944 | tf_op jit(solution)/shard_map/ppermute | solution.py:1033
  304.8 7.0 %collective-permute-done.49.refs_1_ = bf16[4,96,384]{2,1,0:T(8,128)(2,1)S(1)} collective-permute-done((bf16[4,96,384]{2,1,0:T(8,128)(2,1)S(1)}, bf16[4,96,384]{2,1,0:T(8,128)(2,1)S(1)}, u32[]{:S(2)}, u32[]{:S(2)}) %collective-permute-start.49) | collective-permute-done | bytes 294944 | tf_op jit(solution)/shard_map/ppermute | solution.py:1033
  315.2 4.6 %collective-permute-done.51.refs_3_ = bf16[4,96,384]{2,1,0:T(8,128)(2,1)S(1)} collective-permute-done((bf16[4,96,384]{2,1,0:T(8,128)(2,1)S(1)}, bf16[4,96,384]{2,1,0:T(8,128)(2,1)S(1)}, u32[]{:S(2)}, u32[]{:S(2)}) %collective-permute-start.51) | collective-permute-done | bytes 294944 | tf_op jit(solution)/shard_map/ppermute | solution.py:1033
  323.5 4.7 %last_products.1 = (f32[128,3072]{1,0:T(8,128)}, f32[1,128]{1,0:T(1,128)}, f32[32,1024]{1,0:T(8,128)}, f32[8,128]{1,0:T(8,128)S(1)}) custom-call(s32[6]{0:T(128)S(1)} %stack.27.places.s, bf16[4,384,384]{2,1,0:T(8,128)(2,1)S(1)} %stack_rows.1.mine, bf16[4,384,384]{2,1,0:T(8,128)(2,1)S(1)} %collective-permute-done.52.other, bf16[256,1024]{1,0:T(8,128)(2,1)S(1)} %copy-done.36, ...), custom_call_target="tpu_custom_call" | custom-call | flops 1000 | bytes 1000 | tf_op jit(solution)/shard_map/last_products/pallas_call | solution.py:1497
  (260 shorter events, 140.8 us)
Async XLA Ops:
  72.2 16.6 %collective-permute-start.4 = (bf16[4,256,1024]{2,1,0:T(8,128)(2,1)S(1)}, bf16[4,256,1024]{2,1,0:T(8,128)(2,1)S(1)}, u32[]{:S(2)}, u32[]{:S(2)}) collective-permute-start(bf16[4,256,1024]{2,1,0:T(8,128)(2,1)S(1)} %get-tuple-element.165), channel_id=1, source_target_pairs={{0,1},{1,0},{2,3},{3,2},{4,5},{5,4},{6,7},{7,6},{8,9},{9,8},{10,11... | collective-permute-start | bytes 6291464 | tf_op jit(solution)/shard_map/ppermute | solution.py:1033
  72.7 14.6 %collective-permute-start.5 = (bf16[4,64,1024]{2,1,0:T(8,128)(2,1)S(1)}, bf16[4,64,1024]{2,1,0:T(8,128)(2,1)S(1)}, u32[]{:S(2)}, u32[]{:S(2)}) collective-permute-start(bf16[4,64,1024]{2,1,0:T(8,128)(2,1)S(1)} %get-tuple-element.166), channel_id=1, source_target_pairs={{0,16},{8,24},{16,0},{24,8},{1,17},{9,25},{17,1},{25,9},{2,18},{10... | collective-permute-start | bytes 1572872 | tf_op jit(solution)/shard_map/ppermute | solution.py:1033
  89.9 20.1 %collective-permute-start.7 = (bf16[4,256,1024]{2,1,0:T(8,128)(2,1)}, bf16[4,256,1024]{2,1,0:T(8,128)(2,1)S(1)}, u32[]{:S(2)}, u32[]{:S(2)}) collective-permute-start(bf16[4,256,1024]{2,1,0:T(8,128)(2,1)} %get-tuple-element.175), channel_id=1, source_target_pairs={{0,1},{1,0},{2,3},{3,2},{4,5},{5,4},{6,7},{7,6},{8,9},{9,8},{10,11... | collective-permute-start | bytes 6291464 | tf_op jit(solution)/shard_map/ppermute | solution.py:1033
  90.0 20.0 %collective-permute-start.8 = (bf16[4,96,1024]{2,1,0:T(8,128)(2,1)S(1)}, bf16[4,96,1024]{2,1,0:T(8,128)(2,1)S(1)}, u32[]{:S(2)}, u32[]{:S(2)}) collective-permute-start(bf16[4,96,1024]{2,1,0:T(8,128)(2,1)S(1)} %get-tuple-element.176), channel_id=1, source_target_pairs={{0,16},{8,24},{16,0},{24,8},{1,17},{9,25},{17,1},{25,9},{2,18},{10... | collective-permute-start | bytes 2359304 | tf_op jit(solution)/shard_map/ppermute | solution.py:1033
  90.4 19.6 %collective-permute-start.9 = (bf16[4,96,1024]{2,1,0:T(8,128)(2,1)S(1)}, bf16[4,96,1024]{2,1,0:T(8,128)(2,1)S(1)}, u32[]{:S(2)}, u32[]{:S(2)}) collective-permute-start(bf16[4,96,1024]{2,1,0:T(8,128)(2,1)S(1)} %get-tuple-element.168.rest_0_), channel_id=1, source_target_pairs={{0,8},{8,0},{16,24},{24,16},{1,9},{9,1},{17,25},{25,17},{2,10},{10... | collective-permute-start | bytes 2359304 | tf_op jit(solution)/shard_map/ppermute | solution.py:1033
  113.1 21.5 %collective-permute-start.10 = (bf16[4,256,1024]{2,1,0:T(8,128)(2,1)S(1)}, bf16[4,256,1024]{2,1,0:T(8,128)(2,1)S(1)}, u32[]{:S(2)}, u32[]{:S(2)}) collective-permute-start(bf16[4,256,1024]{2,1,0:T(8,128)(2,1)S(1)} %get-tuple-element.189), channel_id=1, source_target_pairs={{0,1},{1,0},{2,3},{3,2},{4,5},{5,4},{6,7},{7,6},{8,9},{9,8},{10,11... | collective-permute-start | bytes 6291464 | tf_op jit(solution)/shard_map/ppermute | solution.py:1033
  113.2 20.0 %collective-permute-start.11 = (bf16[4,96,1024]{2,1,0:T(8,128)(2,1)S(1)}, bf16[4,96,1024]{2,1,0:T(8,128)(2,1)S(1)}, u32[]{:S(2)}, u32[]{:S(2)}) collective-permute-start(bf16[4,96,1024]{2,1,0:T(8,128)(2,1)S(1)} %get-tuple-element.190), channel_id=1, source_target_pairs={{0,16},{8,24},{16,0},{24,8},{1,17},{9,25},{17,1},{25,9},{2,18},{10... | collective-permute-start | bytes 2359304 | tf_op jit(solution)/shard_map/ppermute | solution.py:1033
  115.0 19.6 %collective-permute-start.12 = (bf16[4,96,1024]{2,1,0:T(8,128)(2,1)S(1)}, bf16[4,96,1024]{2,1,0:T(8,128)(2,1)S(1)}, u32[]{:S(2)}, u32[]{:S(2)}) collective-permute-start(bf16[4,96,1024]{2,1,0:T(8,128)(2,1)S(1)} %get-tuple-element.178.rest_0_), channel_id=1, source_target_pairs={{0,8},{8,0},{16,24},{24,16},{1,9},{9,1},{17,25},{25,17},{2,10},{10... | collective-permute-start | bytes 2359304 | tf_op jit(solution)/shard_map/ppermute | solution.py:1033
  147.5 20.1 %collective-permute-start.13 = (bf16[4,384,1024]{2,1,0:T(8,128)(2,1)S(1)}, bf16[4,384,1024]{2,1,0:T(8,128)(2,1)S(1)}, u32[]{:S(2)}, u32[]{:S(2)}) collective-permute-start(bf16[4,384,1024]{2,1,0:T(8,128)(2,1)S(1)} %get-tuple-element.198.rest_0_), channel_id=1, source_target_pairs={{0,1},{1,0},{2,3},{3,2},{4,5},{5,4},{6,7},{7,6},{8,9},{9,8},{10,11... | collective-permute-start | bytes 9437192 | tf_op jit(solution)/shard_map/ppermute | solution.py:1033
  147.6 20.0 %collective-permute-start.14 = (bf16[4,96,1024]{2,1,0:T(8,128)(2,1)S(1)}, bf16[4,96,1024]{2,1,0:T(8,128)(2,1)S(1)}, u32[]{:S(2)}, u32[]{:S(2)}) collective-permute-start(bf16[4,96,1024]{2,1,0:T(8,128)(2,1)S(1)} %get-tuple-element.199), channel_id=1, source_target_pairs={{0,16},{8,24},{16,0},{24,8},{1,17},{9,25},{17,1},{25,9},{2,18},{10... | collective-permute-start | bytes 2359304 | tf_op jit(solution)/shard_map/ppermute | solution.py:1033
  147.9 19.6 %collective-permute-start.15 = (bf16[4,96,1024]{2,1,0:T(8,128)(2,1)S(1)}, bf16[4,96,1024]{2,1,0:T(8,128)(2,1)S(1)}, u32[]{:S(2)}, u32[]{:S(2)}) collective-permute-start(bf16[4,96,1024]{2,1,0:T(8,128)(2,1)S(1)} %get-tuple-element.191.rest_0_), channel_id=1, source_target_pairs={{0,8},{8,0},{16,24},{24,16},{1,9},{9,1},{17,25},{25,17},{2,10},{10... | collective-permute-start | bytes 2359304 | tf_op jit(solution)/shard_map/ppermute | solution.py:1033
  169.0 24.8 %collective-permute-start.17 = (bf16[4,128,1024]{2,1,0:T(8,128)(2,1)S(1)}, bf16[4,128,1024]{2,1,0:T(8,128)(2,1)S(1)}, u32[]{:S(2)}, u32[]{:S(2)}) collective-permute-start(bf16[4,128,1024]{2,1,0:T(8,128)(2,1)S(1)} %get-tuple-element.209), channel_id=1, source_target_pairs={{0,16},{8,24},{16,0},{24,8},{1,17},{9,25},{17,1},{25,9},{2,18},{10... | collective-permute-start | bytes 3145736 | tf_op jit(solution)/shard_map/ppermute | solution.py:1033
  170.8 24.1 %collective-permute-start.18 = (bf16[4,128,1024]{2,1,0:T(8,128)(2,1)S(1)}, bf16[4,128,1024]{2,1,0:T(8,128)(2,1)S(1)}, u32[]{:S(2)}, u32[]{:S(2)}) collective-permute-start(bf16[4,128,1024]{2,1,0:T(8,128)(2,1)S(1)} %get-tuple-element.203.rest_0_), channel_id=1, source_target_pairs={{0,8},{8,0},{16,24},{24,16},{1,9},{9,1},{17,25},{25,17},{2,10},{10... | collective-permute-start | bytes 3145736 | tf_op jit(solution)/shard_map/ppermute | solution.py:1033
  172.3 16.4 %collective-permute-start.19 = (bf16[1,128,1024]{2,1,0:T(8,128)(2,1)S(1)}, bf16[1,128,1024]{2,1,0:T(8,128)(2,1)S(1)}, u32[]{:S(2)}, u32[]{:S(2)}) collective-permute-start(bf16[1,128,1024]{2,1,0:T(8,128)(2,1)S(1)} %get-tuple-element.210), channel_id=1, source_target_pairs={{0,4},{1,5},{2,6},{3,7},{4,0},{5,1},{6,2},{7,3},{8,12},{9,13},{10,... | collective-permute-start | bytes 786440 | tf_op jit(solution)/shard_map/ppermute | solution.py:1033
  196.9 21.6 %collective-permute-start.20 = (bf16[4,128,1024]{2,1,0:T(8,128)(2,1)S(1)}, bf16[4,128,1024]{2,1,0:T(8,128)(2,1)S(1)}, u32[]{:S(2)}, u32[]{:S(2)}) collective-permute-start(bf16[4,128,1024]{2,1,0:T(8,128)(2,1)S(1)} %get-tuple-element.212), channel_id=1, source_target_pairs={{0,1},{1,0},{2,3},{3,2},{4,5},{5,4},{6,7},{7,6},{8,9},{9,8},{10,11... | collective-permute-start | bytes 3145736 | tf_op jit(solution)/shard_map/ppermute | solution.py:1033
  197.0 21.5 %collective-permute-start.21 = (bf16[2,128,1024]{2,1,0:T(8,128)(2,1)S(1)}, bf16[2,128,1024]{2,1,0:T(8,128)(2,1)S(1)}, u32[]{:S(2)}, u32[]{:S(2)}) collective-permute-start(bf16[2,128,1024]{2,1,0:T(8,128)(2,1)S(1)} %get-tuple-element.214), channel_id=1, source_target_pairs={{0,2},{1,3},{2,0},{3,1},{4,6},{5,7},{6,4},{7,5},{8,10},{9,11},{10,... | collective-permute-start | bytes 1572872 | tf_op jit(solution)/shard_map/ppermute | solution.py:1033
  199.6 17.4 %collective-permute-start.22 = (bf16[4,48,1024]{2,1,0:T(8,128)(2,1)S(1)}, bf16[4,48,1024]{2,1,0:T(8,128)(2,1)S(1)}, u32[]{:S(2)}, u32[]{:S(2)}) collective-permute-start(bf16[4,48,1024]{2,1,0:T(8,128)(2,1)S(1)} %get-tuple-element.215.refs_12_), channel_id=1, source_target_pairs={{0,8},{8,0},{16,24},{24,16},{1,9},{9,1},{17,25},{25,17},{2,10},{10... | collective-permute-start | bytes 1179656 | tf_op jit(solution)/shard_map/ppermute | solution.py:1033
  201.1 17.3 %collective-permute-start.23 = (bf16[4,48,1024]{2,1,0:T(8,128)(2,1)S(1)}, bf16[4,48,1024]{2,1,0:T(8,128)(2,1)S(1)}, u32[]{:S(2)}, u32[]{:S(2)}) collective-permute-start(bf16[4,48,1024]{2,1,0:T(8,128)(2,1)S(1)} %get-tuple-element.217), channel_id=1, source_target_pairs={{0,16},{8,24},{16,0},{24,8},{1,17},{9,25},{17,1},{25,9},{2,18},{10... | collective-permute-start | bytes 1179656 | tf_op jit(solution)/shard_map/ppermute | solution.py:1033
  201.7 14.7 %collective-permute-start.27 = (bf16[1,128,1024]{2,1,0:T(8,128)(2,1)S(1)}, bf16[1,128,1024]{2,1,0:T(8,128)(2,1)S(1)}, u32[]{:S(2)}, u32[]{:S(2)}) collective-permute-start(bf16[1,128,1024]{2,1,0:T(8,128)(2,1)S(1)} %get-tuple-element.230.refs_0_), channel_id=1, source_target_pairs={{0,8},{8,0},{16,24},{24,16},{1,9},{9,1},{17,25},{25,17},{2,10},{10... | collective-permute-start | bytes 786440 | tf_op jit(solution)/shard_map/ppermute | solution.py:1033
  216.4 25.1 %collective-permute-start.28 = (bf16[1,128,1024]{2,1,0:T(8,128)(2,1)S(1)}, bf16[1,128,1024]{2,1,0:T(8,128)(2,1)S(1)}, u32[]{:S(2)}, u32[]{:S(2)}) collective-permute-start(bf16[1,128,1024]{2,1,0:T(8,128)(2,1)S(1)} %get-tuple-element.230.refs_0_), channel_id=1, source_target_pairs={{0,16},{8,24},{16,0},{24,8},{1,17},{9,25},{17,1},{25,9},{2,18},{10... | collective-permute-start | bytes 786440 | tf_op jit(solution)/shard_map/ppermute | solution.py:1033
  217.0 24.5 %collective-permute-start.29 = (bf16[1,128,1024]{2,1,0:T(8,128)(2,1)S(1)}, bf16[1,128,1024]{2,1,0:T(8,128)(2,1)S(1)}, u32[]{:S(2)}, u32[]{:S(2)}) collective-permute-start(bf16[1,128,1024]{2,1,0:T(8,128)(2,1)S(1)} %collective-permute-done.27.refs_28_.refs_1_), channel_id=1, source_target_pairs={{0,16},{8,24},{16,0},{24,8},{1,17},{9,25},{17,1},{25,9},{2,18},{10... | collective-permute-start | bytes 786440 | tf_op jit(solution)/shard_map/ppermute | solution.py:1033
  219.5 22.1 %collective-permute-start.24 = (bf16[4,32,1024]{2,1,0:T(8,128)(2,1)S(1)}, bf16[4,32,1024]{2,1,0:T(8,128)(2,1)S(1)}, u32[]{:S(2)}, u32[]{:S(2)}) collective-permute-start(bf16[4,32,1024]{2,1,0:T(8,128)(2,1)S(1)} %get-tuple-element.228), channel_id=1, source_target_pairs={{0,16},{8,24},{16,0},{24,8},{1,17},{9,25},{17,1},{25,9},{2,18},{10... | collective-permute-start | bytes 786440 | tf_op jit(solution)/shard_map/ppermute | solution.py:1033
  220.2 21.5 %collective-permute-start.25 = (bf16[4,32,1024]{2,1,0:T(8,128)(2,1)S(1)}, bf16[4,32,1024]{2,1,0:T(8,128)(2,1)S(1)}, u32[]{:S(2)}, u32[]{:S(2)}) collective-permute-start(bf16[4,32,1024]{2,1,0:T(8,128)(2,1)S(1)} %get-tuple-element.218.refs_12_), channel_id=1, source_target_pairs={{0,8},{8,0},{16,24},{24,16},{1,9},{9,1},{17,25},{25,17},{2,10},{10... | collective-permute-start | bytes 786440 | tf_op jit(solution)/shard_map/ppermute | solution.py:1033
  221.7 20.0 %collective-permute-start.26 = (bf16[1,128,1024]{2,1,0:T(8,128)(2,1)S(1)}, bf16[1,128,1024]{2,1,0:T(8,128)(2,1)S(1)}, u32[]{:S(2)}, u32[]{:S(2)}) collective-permute-start(bf16[1,128,1024]{2,1,0:T(8,128)(2,1)S(1)} %get-tuple-element.229), channel_id=1, source_target_pairs={{0,4},{1,5},{2,6},{3,7},{4,0},{5,1},{6,2},{7,3},{8,12},{9,13},{10,... | collective-permute-start | bytes 786440 | tf_op jit(solution)/shard_map/ppermute | solution.py:1033
  (92 other events, 833.4 us)

commit v2 on v1

--- a/solution.py
+++ b/solution.py
@@ -1009,7 +1009,9 @@
         states_back_kernel,
         "states_back",
         (
-            *stays(gsk, gsv, v.state_kv_weight, v.state_normed, v.state_unit, v.state_inv),
+            *stays(gsk, gsv),
+            v.state_kv_weight,
+            *stays(v.state_normed, v.state_unit, v.state_inv),
             v.state_gain,
             *stays(v.forget_slope),
             v.forget,

time: 335 us -> 334 us (level)
    unnamed x126 -> x128, local copies, waits for them, and re-layouts: 10.3 us -> 10.4 us
  transfers between devices with their start and end apart: 53 -> 53, of which waited for: 25 -> 28; matrix products, arithmetic and copies ran while one was open for 0% -> 0% of each run, Pallas kernels for 29% -> 29%
where the time goes in v2:
time: 334 us; the launch traced here: 328 us
  Pallas kernels  165 us (49%)
  waiting for transfers between devices  86 us (26%)
  starting transfers between devices  61.5 us (18%)
  local copies, waits for them, and re-layouts  12 us (4%)
    ppermute x53, waiting for transfers between devices, permute(): return lax.ppermute(value, axis, [(i, to(i)) for i in range(size)])  86 us
    ppermute x53, starting transfers between devices, permute(): return lax.ppermute(value, axis, [(i, to(i)) for i in range(size)])  61.5 us
    pallas_call x4, Pallas kernels, mlp_packed(): pl.pallas_call(mlp_packed_kernel, grid_spec=pltpu.PrefetchScalarGridSpec(...  41.1 us
    pallas_call x2, Pallas kernels, token_backward(): pl.pallas_call(functools.partial(each_head, token_backward_kernel, heads,...  24.2 us
    pallas_call x15, Pallas kernels, blend(): pl.pallas_call(kernel, grid_spec=pltpu.PrefetchScalarGridSpec(num_scalar_...  17.9 us
    pallas_call x1, Pallas kernels, attention_forward(): pl.pallas_call(functools.partial(each_head, attention_forward_kernel, hea...  15.4 us
    pallas_call x4, Pallas kernels, single(): pl.pallas_call(kernel, grid=(1,), in_specs=[one_block(a) for a in ins] +...  12.2 us
    pallas_call x1, Pallas kernels, state_backward(): pl.pallas_call(functools.partial(each_head, state_backward_kernel, heads,...  10.8 us
  transfers between devices with their start and end apart: 53, of which 28 were waited for; matrix products, arithmetic and copies ran while one was open for 0% of the time, Pallas kernels for 29%

profile of v2, /device:TPU:0, one launch (start us, length us, event | category | flops | bytes accessed | tf_op | source)
XLA Modules:
  0.0 328.5 jit_solution(13541571898878542892)
XLA Ops:
  18.6 6.2 %summary_forward.1 = (f32[512,1024]{1,0:T(8,128)S(1)}, f32[512,1024]{1,0:T(8,128)}, f32[2,8,128]{2,1,0:T(8,128)S(1)}) custom-call(s32[2]{0:T(128)S(1)} %get-tuple-element.143.span, bf16[512,1024]{1,0:T(8,128)(2,1)S(1)} %copy-done.19, bf16[256,3072]{1,0:T(8,128)(2,1)S(1)} %table_more.3.rest_0_.kt.vt.refs_3_.refs_4_.refs_5_.refs_1_, ...), custom_call_target="tpu_custom_call" | custom-call | flops 1000 | bytes 1000 | tf_op jit(solution)/shard_map/summary_forward/pallas_call | solution.py:195
  24.8 4.9 %states_forward.1 = (f32[512,1024]{1,0:T(8,128)}, f32[512,128]{1,0:T(8,128)}, bf16[512,1024]{1,0:T(8,128)(2,1)}, bf16[512,2048]{1,0:T(8,128)(2,1)S(1)}) custom-call(f32[512,1024]{1,0:T(8,128)S(1)} %get-tuple-element.147.states, f32[1,1024]{1,0:T(1,128)S(1)} %bitcast.53, bf16[1024,2048]{1,0:T(8,128)(2,1)S(1)} %copy-done.13), custom_call_target="tpu_custom_call" | custom-call | flops 1000 | bytes 1000 | tf_op jit(solution)/shard_map/states_forward/pallas_call | solution.py:891
  29.8 15.4 %attention_forward.1 = (bf16[512,1024]{1,0:T(8,128)(2,1)S(1)}, f32[8,1,512]{2,1,0:T(1,128)S(1)}) custom-call(s32[1]{0:T(128)} %get-tuple-element.140.refs_0_, bf16[1024,256]{1,0:T(8,128)(2,1)S(1)} %get-tuple-element.141.refs_1_.pick.refs_0_, bf16[256,1024]{1,0:T(8,128)(2,1)S(1)} %get-tuple-element.142.refs_2_, ...), custom_call_target="tpu_custom_call" | custom-call | flops 1000 | bytes 1000 | tf_op jit(solution)/shard_map/attention_forward/pallas_call | solution.py:410
  45.3 4.1 %residual_forward.1 = (f32[512,1024]{1,0:T(8,128)S(1)}, f32[512,1024]{1,0:T(8,128)}, f32[512,128]{1,0:T(8,128)}, bf16[512,1024]{1,0:T(8,128)(2,1)S(1)}, bf16[2,512,512]{2,1,0:T(8,128)(2,1)S(1)}) custom-call(s32[6]{0:T(128)S(1)} %stack.27.places.s, bf16[512,1024]{1,0:T(8,128)(2,1)S(1)} %get-tuple-element.150.mixed.refs_5_, bf16[1024,1024]{1,0:T(8,128)(2,1)S(1)} %copy-done.29, ...), custom_call_target="tpu_custom_call" | custom-call | flops 1000 | bytes 1000 | tf_op jit(solution)/shard_map/residual_forward/pallas_call | solution.py:943
  51.0 10.0 %feed_forward.4 = (bf16[4,256,1024]{2,1,0:T(8,128)(2,1)S(1)}, bf16[4,256,1024]{2,1,0:T(8,128)(2,1)S(1)}, f32[512,1024]{1,0:T(8,128)S(1)}, f32[512,1024]{1,0:T(8,128)S(1)}) custom-call(s32[6]{0:T(128)S(1)} %stack.27.places.s, bf16[512,1024]{1,0:T(8,128)(2,1)S(1)} %get-tuple-element.151.x, bf16[2,512,512]{2,1,0:T(8,128)(2,1)S(1)} %get-tuple-element.152.xs, ...), custom_call_target="tpu_custom_call" | custom-call | flops 1000 | bytes 1000 | tf_op jit(solution)/shard_map/feed_forward/pallas_call | solution.py:746
  62.0 10.2 %feed_forward.5 = (bf16[4,256,1024]{2,1,0:T(8,128)(2,1)S(1)}, bf16[4,256,1024]{2,1,0:T(8,128)(2,1)S(1)}, f32[512,1024]{1,0:T(8,128)S(1)}, f32[512,1024]{1,0:T(8,128)S(1)}) custom-call(s32[6]{0:T(128)S(1)} %stack.27.places.s, bf16[512,1024]{1,0:T(8,128)(2,1)S(1)} %get-tuple-element.151.x, bf16[2,512,512]{2,1,0:T(8,128)(2,1)S(1)} %get-tuple-element.152.xs, ...), custom_call_target="tpu_custom_call" | custom-call | flops 1000 | bytes 1000 | tf_op jit(solution)/shard_map/feed_forward/pallas_call | solution.py:746
  76.3 11.0 %feed_forward.6 = (bf16[4,256,1024]{2,1,0:T(8,128)(2,1)}, bf16[4,256,1024]{2,1,0:T(8,128)(2,1)S(1)}, f32[512,1024]{1,0:T(8,128)S(1)}, f32[512,1024]{1,0:T(8,128)S(1)}) custom-call(s32[6]{0:T(128)S(1)} %stack.27.places.s, bf16[512,1024]{1,0:T(8,128)(2,1)S(1)} %get-tuple-element.151.x, bf16[2,512,512]{2,1,0:T(8,128)(2,1)S(1)} %get-tuple-element.152.xs, ...), custom_call_target="tpu_custom_call" | custom-call | flops 1000 | bytes 1000 | tf_op jit(solution)/shard_map/feed_forward/pallas_call | solution.py:746
  93.7 10.0 %feed_forward.7 = (bf16[4,256,1024]{2,1,0:T(8,128)(2,1)S(1)}, bf16[4,256,1024]{2,1,0:T(8,128)(2,1)S(1)}, f32[512,1024]{1,0:T(8,128)S(1)}, f32[512,1024]{1,0:T(8,128)S(1)}) custom-call(s32[6]{0:T(128)S(1)} %stack.27.places.s, bf16[512,1024]{1,0:T(8,128)(2,1)S(1)} %get-tuple-element.151.x, bf16[2,512,512]{2,1,0:T(8,128)(2,1)S(1)} %copy-done.12, ...), custom_call_target="tpu_custom_call" | custom-call | flops 1000 | bytes 1000 | tf_op jit(solution)/shard_map/feed_forward/pallas_call | solution.py:746
  122.3 10.8 %state_backward.1 = (bf16[512,1024]{1,0:T(8,128)(2,1)}, bf16[512,1024]{1,0:T(8,128)(2,1)}, f32[8,128,512]{2,1,0:T(8,128)S(1)}, f32[8,1,512]{2,1,0:T(1,128)S(1)}) custom-call(bf16[1024,256]{1,0:T(8,128)(2,1)S(1)} %copy-done.10, bf16[256,3072]{1,0:T(8,128)(2,1)S(1)} %table_more.3.rest_0_.kt.vt.refs_3_.refs_4_.refs_5_.refs_1_, bf16[512,2048]{1,0:T(8,128)(2,1)S(1)} %copy-done.5, ...), custom_call_target="tpu_custom_call" | custom-call | flops 1000 | bytes 1000 | tf_op jit(solution)/shard_map/state_backward/pallas_call | solution.py:484
  136.8 8.6 %states_back.1 = (bf16[1024,1024]{1,0:T(8,128)(2,1)S(1)}, bf16[1024,1024]{1,0:T(8,128)(2,1)S(1)}, f32[1,1024]{1,0:T(1,128)S(1)}, f32[512,1024]{1,0:T(8,128)S(1)}, f32[1,1024]{1,0:T(1,128)S(1)}) custom-call(bf16[512,1024]{1,0:T(8,128)(2,1)} %get-tuple-element.182.gsk, bf16[512,1024]{1,0:T(8,128)(2,1)} %get-tuple-element.183.gsv, ...), custom_call_target="tpu_custom_call" | custom-call | flops 1000 | bytes 1000 | tf_op jit(solution)/shard_map/states_back/pallas_call | solution.py:782
  154.4 8.8 %collective-permute-done.16.refs_11_.refs_15_.refs_39_ = bf16[2,128,1024]{2,1,0:T(8,128)(2,1)S(1)} collective-permute-done((bf16[2,128,1024]{2,1,0:T(8,128)(2,1)S(1)}, bf16[2,128,1024]{2,1,0:T(8,128)(2,1)S(1)}, u32[]{:S(2)}, u32[]{:S(2)}) %collective-permute-start.16) | collective-permute-done | bytes 524320 | tf_op jit(solution)/shard_map/ppermute | solution.py:1035
  171.3 5.6 %collective-permute-start.19 = (bf16[1,128,1024]{2,1,0:T(8,128)(2,1)S(1)}, bf16[1,128,1024]{2,1,0:T(8,128)(2,1)S(1)}, u32[]{:S(2)}, u32[]{:S(2)}) collective-permute-start(bf16[1,128,1024]{2,1,0:T(8,128)(2,1)S(1)} %get-tuple-element.210), channel_id=1, source_target_pairs={{0,4},{1,5},{2,6},{3,7},{4,0},{5,1},{6,2},{7,3},{8,12},{9,13},{10,... | collective-permute-start | bytes 786440 | tf_op jit(solution)/shard_map/ppermute | solution.py:1035
  181.2 6.5 %collective-permute-done.19.refs_40_.refs_43_ = bf16[1,128,1024]{2,1,0:T(8,128)(2,1)S(1)} collective-permute-done((bf16[1,128,1024]{2,1,0:T(8,128)(2,1)S(1)}, bf16[1,128,1024]{2,1,0:T(8,128)(2,1)S(1)}, u32[]{:S(2)}, u32[]{:S(2)}) %collective-permute-start.19) | collective-permute-done | bytes 262176 | tf_op jit(solution)/shard_map/ppermute | solution.py:1035
  187.7 5.1 %collective-permute-done.17.refs_2_.refs_17_.refs_33_.refs_42_.refs_12_.refs_20_ = bf16[4,128,1024]{2,1,0:T(8,128)(2,1)S(1)} collective-permute-done((bf16[4,128,1024]{2,1,0:T(8,128)(2,1)S(1)}, bf16[4,128,1024]{2,1,0:T(8,128)(2,1)S(1)}, u32[]{:S(2)}, u32[]{:S(2)}) %collective-permute-start.17) | collective-permute-done | bytes 1048608 | tf_op jit(solution)/shard_map/ppermute | solution.py:1035
  201.3 12.0 %token_backward.2 = (f32[8,256,384]{2,1,0:T(8,128)S(1)}, f32[8,1,128]{2,1,0:T(1,128)S(1)}) custom-call(s32[1]{0:T(128)} %get-tuple-element.140.refs_0_, bf16[1024,256]{1,0:T(8,128)(2,1)S(1)} %copy-done.10, bf16[256,1024]{1,0:T(8,128)(2,1)S(1)} %copy-done.39, bf16[256,3072]{1,0:T(8,128)(2,1)S(1)} %table_more.3.rest_0_.kt.vt.refs_3_.refs_4_.refs_5_.refs_1_, ...), custom_call_target="tpu_custom_call" | custom-call | flops 1000 | bytes 1000 | tf_op jit(solution)/shard_map/token_backward/pallas_call | solution.py:594
  220.6 6.5 %collective-permute-start.26 = (bf16[1,128,1024]{2,1,0:T(8,128)(2,1)S(1)}, bf16[1,128,1024]{2,1,0:T(8,128)(2,1)S(1)}, u32[]{:S(2)}, u32[]{:S(2)}) collective-permute-start(bf16[1,128,1024]{2,1,0:T(8,128)(2,1)S(1)} %get-tuple-element.229), channel_id=1, source_target_pairs={{0,4},{1,5},{2,6},{3,7},{4,0},{5,1},{6,2},{7,3},{8,12},{9,13},{10,... | collective-permute-start | bytes 786440 | tf_op jit(solution)/shard_map/ppermute | solution.py:1035
  227.2 12.2 %token_backward.3 = (f32[8,256,384]{2,1,0:T(8,128)S(1)}, f32[8,1,128]{2,1,0:T(1,128)S(1)}) custom-call(s32[1]{0:T(128)} %get-tuple-element.140.refs_0_, bf16[1024,256]{1,0:T(8,128)(2,1)S(1)} %copy-done.10, bf16[256,1024]{1,0:T(8,128)(2,1)S(1)} %copy-done.39, ...), custom_call_target="tpu_custom_call", output_to_operand_aliasing={{0}: (13, {}), {1}: (14, {})} | custom-call | flops 1000 | bytes 1000 | tf_op jit(solution)/shard_map/token_backward/pallas_call | solution.py:594
  249.2 4.5 %collective-permute-done.33.refs_21_.refs_24_.refs_9_ = bf16[2,96,1024]{2,1,0:T(8,128)(2,1)S(1)} collective-permute-done((bf16[2,96,1024]{2,1,0:T(8,128)(2,1)S(1)}, bf16[2,96,1024]{2,1,0:T(8,128)(2,1)S(1)}, u32[]{:S(2)}, u32[]{:S(2)}) %collective-permute-start.33) | collective-permute-done | bytes 393248 | tf_op jit(solution)/shard_map/ppermute | solution.py:1035
  258.7 4.7 %collective-permute-done.36.refs_7_.refs_10_.refs_12_ = bf16[2,32,1024]{2,1,0:T(8,128)(2,1)S(1)} collective-permute-done((bf16[2,32,1024]{2,1,0:T(8,128)(2,1)S(1)}, bf16[2,32,1024]{2,1,0:T(8,128)(2,1)S(1)}, u32[]{:S(2)}, u32[]{:S(2)}) %collective-permute-start.36) | collective-permute-done | bytes 131104 | tf_op jit(solution)/shard_map/ppermute | solution.py:1035
  271.1 4.9 %collective-permute-done.43.refs_19_.refs_7_ = bf16[1,128,1024]{2,1,0:T(8,128)(2,1)S(1)} collective-permute-done((bf16[1,128,1024]{2,1,0:T(8,128)(2,1)S(1)}, bf16[1,128,1024]{2,1,0:T(8,128)(2,1)S(1)}, u32[]{:S(2)}, u32[]{:S(2)}) %collective-permute-start.43) | collective-permute-done | bytes 262176 | tf_op jit(solution)/shard_map/ppermute | solution.py:1035
  279.7 6.9 %collective-permute-done.44.refs_1_.refs_2_ = bf16[4,96,384]{2,1,0:T(8,128)(2,1)S(1)} collective-permute-done((bf16[4,96,384]{2,1,0:T(8,128)(2,1)S(1)}, bf16[4,96,384]{2,1,0:T(8,128)(2,1)S(1)}, u32[]{:S(2)}, u32[]{:S(2)}) %collective-permute-start.44) | collective-permute-done | bytes 294944 | tf_op jit(solution)/shard_map/ppermute | solution.py:1035
  303.8 7.0 %collective-permute-done.49.refs_1_ = bf16[4,96,384]{2,1,0:T(8,128)(2,1)S(1)} collective-permute-done((bf16[4,96,384]{2,1,0:T(8,128)(2,1)S(1)}, bf16[4,96,384]{2,1,0:T(8,128)(2,1)S(1)}, u32[]{:S(2)}, u32[]{:S(2)}) %collective-permute-start.49) | collective-permute-done | bytes 294944 | tf_op jit(solution)/shard_map/ppermute | solution.py:1035
  314.2 4.6 %collective-permute-done.51.refs_3_ = bf16[4,96,384]{2,1,0:T(8,128)(2,1)S(1)} collective-permute-done((bf16[4,96,384]{2,1,0:T(8,128)(2,1)S(1)}, bf16[4,96,384]{2,1,0:T(8,128)(2,1)S(1)}, u32[]{:S(2)}, u32[]{:S(2)}) %collective-permute-start.51) | collective-permute-done | bytes 294944 | tf_op jit(solution)/shard_map/ppermute | solution.py:1035
  322.5 4.7 %last_products.1 = (f32[128,3072]{1,0:T(8,128)}, f32[1,128]{1,0:T(1,128)}, f32[32,1024]{1,0:T(8,128)}, f32[8,128]{1,0:T(8,128)S(1)}) custom-call(s32[6]{0:T(128)S(1)} %stack.27.places.s, bf16[4,384,384]{2,1,0:T(8,128)(2,1)S(1)} %stack_rows.1.mine, bf16[4,384,384]{2,1,0:T(8,128)(2,1)S(1)} %collective-permute-done.52.other, bf16[256,1024]{1,0:T(8,128)(2,1)S(1)} %copy-done.37, ...), custom_call_target="tpu_custom_call" | custom-call | flops 1000 | bytes 1000 | tf_op jit(solution)/shard_map/last_products/pallas_call | solution.py:1499
  (262 shorter events, 141.0 us)
Async XLA Ops:
  73.1 15.7 %collective-permute-start.4 = (bf16[4,256,1024]{2,1,0:T(8,128)(2,1)S(1)}, bf16[4,256,1024]{2,1,0:T(8,128)(2,1)S(1)}, u32[]{:S(2)}, u32[]{:S(2)}) collective-permute-start(bf16[4,256,1024]{2,1,0:T(8,128)(2,1)S(1)} %get-tuple-element.165), channel_id=1, source_target_pairs={{0,1},{1,0},{2,3},{3,2},{4,5},{5,4},{6,7},{7,6},{8,9},{9,8},{10,11... | collective-permute-start | bytes 6291464 | tf_op jit(solution)/shard_map/ppermute | solution.py:1035
  89.9 20.3 %collective-permute-start.7 = (bf16[4,256,1024]{2,1,0:T(8,128)(2,1)}, bf16[4,256,1024]{2,1,0:T(8,128)(2,1)S(1)}, u32[]{:S(2)}, u32[]{:S(2)}) collective-permute-start(bf16[4,256,1024]{2,1,0:T(8,128)(2,1)} %get-tuple-element.175), channel_id=1, source_target_pairs={{0,1},{1,0},{2,3},{3,2},{4,5},{5,4},{6,7},{7,6},{8,9},{9,8},{10,11... | collective-permute-start | bytes 6291464 | tf_op jit(solution)/shard_map/ppermute | solution.py:1035
  90.0 20.0 %collective-permute-start.8 = (bf16[4,96,1024]{2,1,0:T(8,128)(2,1)S(1)}, bf16[4,96,1024]{2,1,0:T(8,128)(2,1)S(1)}, u32[]{:S(2)}, u32[]{:S(2)}) collective-permute-start(bf16[4,96,1024]{2,1,0:T(8,128)(2,1)S(1)} %get-tuple-element.176), channel_id=1, source_target_pairs={{0,16},{8,24},{16,0},{24,8},{1,17},{9,25},{17,1},{25,9},{2,18},{10... | collective-permute-start | bytes 2359304 | tf_op jit(solution)/shard_map/ppermute | solution.py:1035
  90.6 19.6 %collective-permute-start.9 = (bf16[4,96,1024]{2,1,0:T(8,128)(2,1)S(1)}, bf16[4,96,1024]{2,1,0:T(8,128)(2,1)S(1)}, u32[]{:S(2)}, u32[]{:S(2)}) collective-permute-start(bf16[4,96,1024]{2,1,0:T(8,128)(2,1)S(1)} %get-tuple-element.168.rest_0_), channel_id=1, source_target_pairs={{0,8},{8,0},{16,24},{24,16},{1,9},{9,1},{17,25},{25,17},{2,10},{10... | collective-permute-start | bytes 2359304 | tf_op jit(solution)/shard_map/ppermute | solution.py:1035
  113.3 21.3 %collective-permute-start.10 = (bf16[4,256,1024]{2,1,0:T(8,128)(2,1)S(1)}, bf16[4,256,1024]{2,1,0:T(8,128)(2,1)S(1)}, u32[]{:S(2)}, u32[]{:S(2)}) collective-permute-start(bf16[4,256,1024]{2,1,0:T(8,128)(2,1)S(1)} %get-tuple-element.189), channel_id=1, source_target_pairs={{0,1},{1,0},{2,3},{3,2},{4,5},{5,4},{6,7},{7,6},{8,9},{9,8},{10,11... | collective-permute-start | bytes 6291464 | tf_op jit(solution)/shard_map/ppermute | solution.py:1035
  113.4 20.0 %collective-permute-start.11 = (bf16[4,96,1024]{2,1,0:T(8,128)(2,1)S(1)}, bf16[4,96,1024]{2,1,0:T(8,128)(2,1)S(1)}, u32[]{:S(2)}, u32[]{:S(2)}) collective-permute-start(bf16[4,96,1024]{2,1,0:T(8,128)(2,1)S(1)} %get-tuple-element.190), channel_id=1, source_target_pairs={{0,16},{8,24},{16,0},{24,8},{1,17},{9,25},{17,1},{25,9},{2,18},{10... | collective-permute-start | bytes 2359304 | tf_op jit(solution)/shard_map/ppermute | solution.py:1035
  115.0 19.6 %collective-permute-start.12 = (bf16[4,96,1024]{2,1,0:T(8,128)(2,1)S(1)}, bf16[4,96,1024]{2,1,0:T(8,128)(2,1)S(1)}, u32[]{:S(2)}, u32[]{:S(2)}) collective-permute-start(bf16[4,96,1024]{2,1,0:T(8,128)(2,1)S(1)} %get-tuple-element.178.rest_0_), channel_id=1, source_target_pairs={{0,8},{8,0},{16,24},{24,16},{1,9},{9,1},{17,25},{25,17},{2,10},{10... | collective-permute-start | bytes 2359304 | tf_op jit(solution)/shard_map/ppermute | solution.py:1035
  146.5 20.3 %collective-permute-start.13 = (bf16[4,384,1024]{2,1,0:T(8,128)(2,1)S(1)}, bf16[4,384,1024]{2,1,0:T(8,128)(2,1)S(1)}, u32[]{:S(2)}, u32[]{:S(2)}) collective-permute-start(bf16[4,384,1024]{2,1,0:T(8,128)(2,1)S(1)} %get-tuple-element.198.rest_0_), channel_id=1, source_target_pairs={{0,1},{1,0},{2,3},{3,2},{4,5},{5,4},{6,7},{7,6},{8,9},{9,8},{10,11... | collective-permute-start | bytes 9437192 | tf_op jit(solution)/shard_map/ppermute | solution.py:1035
  146.5 20.0 %collective-permute-start.14 = (bf16[4,96,1024]{2,1,0:T(8,128)(2,1)S(1)}, bf16[4,96,1024]{2,1,0:T(8,128)(2,1)S(1)}, u32[]{:S(2)}, u32[]{:S(2)}) collective-permute-start(bf16[4,96,1024]{2,1,0:T(8,128)(2,1)S(1)} %get-tuple-element.199), channel_id=1, source_target_pairs={{0,16},{8,24},{16,0},{24,8},{1,17},{9,25},{17,1},{25,9},{2,18},{10... | collective-permute-start | bytes 2359304 | tf_op jit(solution)/shard_map/ppermute | solution.py:1035
  147.1 19.6 %collective-permute-start.15 = (bf16[4,96,1024]{2,1,0:T(8,128)(2,1)S(1)}, bf16[4,96,1024]{2,1,0:T(8,128)(2,1)S(1)}, u32[]{:S(2)}, u32[]{:S(2)}) collective-permute-start(bf16[4,96,1024]{2,1,0:T(8,128)(2,1)S(1)} %get-tuple-element.191.rest_0_), channel_id=1, source_target_pairs={{0,8},{8,0},{16,24},{24,16},{1,9},{9,1},{17,25},{25,17},{2,10},{10... | collective-permute-start | bytes 2359304 | tf_op jit(solution)/shard_map/ppermute | solution.py:1035
  148.6 14.6 %collective-permute-start.16 = (bf16[2,128,1024]{2,1,0:T(8,128)(2,1)S(1)}, bf16[2,128,1024]{2,1,0:T(8,128)(2,1)S(1)}, u32[]{:S(2)}, u32[]{:S(2)}) collective-permute-start(bf16[2,128,1024]{2,1,0:T(8,128)(2,1)S(1)} %get-tuple-element.201), channel_id=1, source_target_pairs={{0,2},{1,3},{2,0},{3,1},{4,6},{5,7},{6,4},{7,5},{8,10},{9,11},{10,... | collective-permute-start | bytes 1572872 | tf_op jit(solution)/shard_map/ppermute | solution.py:1035
  168.2 24.6 %collective-permute-start.17 = (bf16[4,128,1024]{2,1,0:T(8,128)(2,1)S(1)}, bf16[4,128,1024]{2,1,0:T(8,128)(2,1)S(1)}, u32[]{:S(2)}, u32[]{:S(2)}) collective-permute-start(bf16[4,128,1024]{2,1,0:T(8,128)(2,1)S(1)} %get-tuple-element.209), channel_id=1, source_target_pairs={{0,16},{8,24},{16,0},{24,8},{1,17},{9,25},{17,1},{25,9},{2,18},{10... | collective-permute-start | bytes 3145736 | tf_op jit(solution)/shard_map/ppermute | solution.py:1035
  169.8 24.1 %collective-permute-start.18 = (bf16[4,128,1024]{2,1,0:T(8,128)(2,1)S(1)}, bf16[4,128,1024]{2,1,0:T(8,128)(2,1)S(1)}, u32[]{:S(2)}, u32[]{:S(2)}) collective-permute-start(bf16[4,128,1024]{2,1,0:T(8,128)(2,1)S(1)} %get-tuple-element.203.rest_0_), channel_id=1, source_target_pairs={{0,8},{8,0},{16,24},{24,16},{1,9},{9,1},{17,25},{25,17},{2,10},{10... | collective-permute-start | bytes 3145736 | tf_op jit(solution)/shard_map/ppermute | solution.py:1035
  171.3 16.4 %collective-permute-start.19 = (bf16[1,128,1024]{2,1,0:T(8,128)(2,1)S(1)}, bf16[1,128,1024]{2,1,0:T(8,128)(2,1)S(1)}, u32[]{:S(2)}, u32[]{:S(2)}) collective-permute-start(bf16[1,128,1024]{2,1,0:T(8,128)(2,1)S(1)} %get-tuple-element.210), channel_id=1, source_target_pairs={{0,4},{1,5},{2,6},{3,7},{4,0},{5,1},{6,2},{7,3},{8,12},{9,13},{10,... | collective-permute-start | bytes 786440 | tf_op jit(solution)/shard_map/ppermute | solution.py:1035
  195.8 21.6 %collective-permute-start.20 = (bf16[4,128,1024]{2,1,0:T(8,128)(2,1)S(1)}, bf16[4,128,1024]{2,1,0:T(8,128)(2,1)S(1)}, u32[]{:S(2)}, u32[]{:S(2)}) collective-permute-start(bf16[4,128,1024]{2,1,0:T(8,128)(2,1)S(1)} %get-tuple-element.212), channel_id=1, source_target_pairs={{0,1},{1,0},{2,3},{3,2},{4,5},{5,4},{6,7},{7,6},{8,9},{9,8},{10,11... | collective-permute-start | bytes 3145736 | tf_op jit(solution)/shard_map/ppermute | solution.py:1035
  195.9 21.5 %collective-permute-start.21 = (bf16[2,128,1024]{2,1,0:T(8,128)(2,1)S(1)}, bf16[2,128,1024]{2,1,0:T(8,128)(2,1)S(1)}, u32[]{:S(2)}, u32[]{:S(2)}) collective-permute-start(bf16[2,128,1024]{2,1,0:T(8,128)(2,1)S(1)} %get-tuple-element.214), channel_id=1, source_target_pairs={{0,2},{1,3},{2,0},{3,1},{4,6},{5,7},{6,4},{7,5},{8,10},{9,11},{10,... | collective-permute-start | bytes 1572872 | tf_op jit(solution)/shard_map/ppermute | solution.py:1035
  198.6 17.4 %collective-permute-start.22 = (bf16[4,48,1024]{2,1,0:T(8,128)(2,1)S(1)}, bf16[4,48,1024]{2,1,0:T(8,128)(2,1)S(1)}, u32[]{:S(2)}, u32[]{:S(2)}) collective-permute-start(bf16[4,48,1024]{2,1,0:T(8,128)(2,1)S(1)} %get-tuple-element.215.refs_12_), channel_id=1, source_target_pairs={{0,8},{8,0},{16,24},{24,16},{1,9},{9,1},{17,25},{25,17},{2,10},{10... | collective-permute-start | bytes 1179656 | tf_op jit(solution)/shard_map/ppermute | solution.py:1035
  200.1 17.3 %collective-permute-start.23 = (bf16[4,48,1024]{2,1,0:T(8,128)(2,1)S(1)}, bf16[4,48,1024]{2,1,0:T(8,128)(2,1)S(1)}, u32[]{:S(2)}, u32[]{:S(2)}) collective-permute-start(bf16[4,48,1024]{2,1,0:T(8,128)(2,1)S(1)} %get-tuple-element.217), channel_id=1, source_target_pairs={{0,16},{8,24},{16,0},{24,8},{1,17},{9,25},{17,1},{25,9},{2,18},{10... | collective-permute-start | bytes 1179656 | tf_op jit(solution)/shard_map/ppermute | solution.py:1035
  200.7 14.7 %collective-permute-start.27 = (bf16[1,128,1024]{2,1,0:T(8,128)(2,1)S(1)}, bf16[1,128,1024]{2,1,0:T(8,128)(2,1)S(1)}, u32[]{:S(2)}, u32[]{:S(2)}) collective-permute-start(bf16[1,128,1024]{2,1,0:T(8,128)(2,1)S(1)} %get-tuple-element.230.refs_0_), channel_id=1, source_target_pairs={{0,8},{8,0},{16,24},{24,16},{1,9},{9,1},{17,25},{25,17},{2,10},{10... | collective-permute-start | bytes 786440 | tf_op jit(solution)/shard_map/ppermute | solution.py:1035
  215.4 25.2 %collective-permute-start.28 = (bf16[1,128,1024]{2,1,0:T(8,128)(2,1)S(1)}, bf16[1,128,1024]{2,1,0:T(8,128)(2,1)S(1)}, u32[]{:S(2)}, u32[]{:S(2)}) collective-permute-start(bf16[1,128,1024]{2,1,0:T(8,128)(2,1)S(1)} %get-tuple-element.230.refs_0_), channel_id=1, source_target_pairs={{0,16},{8,24},{16,0},{24,8},{1,17},{9,25},{17,1},{25,9},{2,18},{10... | collective-permute-start | bytes 786440 | tf_op jit(solution)/shard_map/ppermute | solution.py:1035
  216.0 24.6 %collective-permute-start.29 = (bf16[1,128,1024]{2,1,0:T(8,128)(2,1)S(1)}, bf16[1,128,1024]{2,1,0:T(8,128)(2,1)S(1)}, u32[]{:S(2)}, u32[]{:S(2)}) collective-permute-start(bf16[1,128,1024]{2,1,0:T(8,128)(2,1)S(1)} %collective-permute-done.27.refs_28_.refs_1_), channel_id=1, source_target_pairs={{0,16},{8,24},{16,0},{24,8},{1,17},{9,25},{17,1},{25,9},{2,18},{10... | collective-permute-start | bytes 786440 | tf_op jit(solution)/shard_map/ppermute | solution.py:1035
  218.5 22.1 %collective-permute-start.24 = (bf16[4,32,1024]{2,1,0:T(8,128)(2,1)S(1)}, bf16[4,32,1024]{2,1,0:T(8,128)(2,1)S(1)}, u32[]{:S(2)}, u32[]{:S(2)}) collective-permute-start(bf16[4,32,1024]{2,1,0:T(8,128)(2,1)S(1)} %get-tuple-element.228), channel_id=1, source_target_pairs={{0,16},{8,24},{16,0},{24,8},{1,17},{9,25},{17,1},{25,9},{2,18},{10... | collective-permute-start | bytes 786440 | tf_op jit(solution)/shard_map/ppermute | solution.py:1035
  219.1 21.5 %collective-permute-start.25 = (bf16[4,32,1024]{2,1,0:T(8,128)(2,1)S(1)}, bf16[4,32,1024]{2,1,0:T(8,128)(2,1)S(1)}, u32[]{:S(2)}, u32[]{:S(2)}) collective-permute-start(bf16[4,32,1024]{2,1,0:T(8,128)(2,1)S(1)} %get-tuple-element.218.refs_12_), channel_id=1, source_target_pairs={{0,8},{8,0},{16,24},{24,16},{1,9},{9,1},{17,25},{25,17},{2,10},{10... | collective-permute-start | bytes 786440 | tf_op jit(solution)/shard_map/ppermute | solution.py:1035
  220.6 20.0 %collective-permute-start.26 = (bf16[1,128,1024]{2,1,0:T(8,128)(2,1)S(1)}, bf16[1,128,1024]{2,1,0:T(8,128)(2,1)S(1)}, u32[]{:S(2)}, u32[]{:S(2)}) collective-permute-start(bf16[1,128,1024]{2,1,0:T(8,128)(2,1)S(1)} %get-tuple-element.229), channel_id=1, source_target_pairs={{0,4},{1,5},{2,6},{3,7},{4,0},{5,1},{6,2},{7,3},{8,12},{9,13},{10,... | collective-permute-start | bytes 786440 | tf_op jit(solution)/shard_map/ppermute | solution.py:1035
  (93 other events, 833.0 us)
